TPU v7x, 32 devices: a whole 2x2x4 slice. The times are simulated.
32 devices in a mesh: seq: 4 (over x, core), exp: 8 (over z, y).
Axes of the slice: x: 2, y: 2, z: 4, core: 2. Of those that a mesh axis runs over, the one named last changes fastest.
Arguments:
- tokens: bfloat16 [2, 8, 512, 1024], P(None, 'exp', 'seq'), may hold values from -3 to 3
- queries: bfloat16 [2, 8, 512, 1024], P(None, 'exp', 'seq'), may hold values from -6 to 6
- key_rows: bfloat16 [2, 8, 512, 1024], P(None, 'exp', 'seq'), may hold values from -6 to 6
- value_rows: bfloat16 [2, 8, 512, 1024], P(None, 'exp', 'seq'), may hold values from -6 to 6
- segments: int32 [2, 8, 512], P(None, 'exp', 'seq'), may hold values from 0 to 3, never falling along the last dimension, each value on 1 to 256 neighbouring positions
- bias_table: float32 [16, 32], replicated, may hold values from -3 to 5
- out_proj: bfloat16 [1024, 1024], replicated, may hold values from -0.75 to 0.75
- router: bfloat16 [1024, 8], replicated, may hold values from -0.1875 to 0.1875
- gate_weight: bfloat16 [8, 1024, 1408], P('exp'), may hold values from -0.1875 to 0.1875
- up_weight: bfloat16 [8, 1024, 1408], P('exp'), may hold values from -0.1875 to 0.1875
- down_weight: bfloat16 [8, 1408, 1024], P('exp'), may hold values from -0.15625 to 0.15625
- old_table: int32 [8], replicated, may hold values from 0 to 7, each once
- new_table: int32 [8], replicated, may hold values from 0 to 7, as said below
- routes_one: int32 [8, 512, 2], P('exp', 'seq'), may hold values from 0 to 7, all different within a row; in each aligned block of 128 rows (0 to 127, 128 to 255, ..., all dimensions but the last counted through in order) at most 40 rows name the same one
- routes_two: int32 [8, 512, 2], P('exp', 'seq'), may hold values from 0 to 7, all different within a row; in each aligned block of 128 rows (0 to 127, 128 to 255, ..., all dimensions but the last counted through in order) at most 40 rows name the same one
Outputs:
- layer_out: bfloat16 [2, 8, 512, 1024], P(None, 'exp', 'seq')
Inputs may be any that keep to these rules, and one draw needn't show every extreme that they name: `old_table`: each position holds a different expert. `new_table`: no expert is served at more than 2 slots, and at least one expert at exactly 2. `routes_one`: the 2 entries of a token differ; in the rows of one device no expert is named more than 40 times, and in some device's rows one is named exactly 40 times. `routes_two`: the 2 entries of a token differ; in the rows of one device no slot is named more than 40 times, and in some device's rows one is named exactly 40 times.
All inputs are finite; a program needn't handle non-finite values.
Results may differ from a plain program's by a relative error of at most 0.006.
Values may be sent and summed in bfloat16 or wider, within the bound.
No kernel may reach another device: no remote copies, remote signals or barrier semaphores. Data moves between devices by JAX's collectives and lax.ppermute only.
A program may use at most 128 MiB of HBM per device.

v0:
```python
import functools

import jax
import jax.numpy as jnp
from jax import lax
from jax.experimental import pallas as pl
from jax.experimental.pallas import tpu as pltpu
from jax.sharding import PartitionSpec as P

WIN_BLOCKS = 4
NBUCK = 32
MAX_SLOTS = 2
ONE_ROW, TWO_ROW, NEW_ROW, OLD_ROW = (2, 4, 6, 7)

score_scale = 0.125
epsilon = 1e-06
masked_score = -1e30

f32 = jnp.float32
bf16 = jnp.bfloat16
NT = (((1,), (1,)), ((), ()))
TN = (((0,), (0,)), ((), ()))
VMEM = pl.BlockSpec(memory_space=pltpu.VMEM)
SMEM = pl.BlockSpec(memory_space=pltpu.SMEM)
ANY = pl.BlockSpec(memory_space=pl.ANY)


def iota(shape, dim):
    return lax.broadcasted_iota(jnp.int32, shape, dim)


def shaped(shape, dtype):
    return jax.ShapeDtypeStruct(shape, dtype)


def passed_along(value, axis, steps):
    count = lax.axis_size(axis)
    return lax.ppermute(value, axis, [(source, source + steps) for source in range(count - steps)])


def swapped(value, axis, mask):
    count = lax.axis_size(axis)
    return lax.ppermute(value, axis, [(source, source ^ mask) for source in range(count)])


def merge_starts(former, latter):
    take_latter = (latter[4] > 0) & ((former[4] == 0) | (latter[3] != former[3]))
    return tuple((jnp.where(take_latter, newer, older) for older, newer in zip(former, latter)))


def latest_start(key_rows, value_rows, segments):
    tok_count, model_width = key_rows.shape
    length, index = (lax.axis_size("seq"), lax.axis_index("seq"))
    last_seg = segments[tok_count - 1]
    lead = jnp.sum((segments < last_seg).astype(jnp.int32))
    one = jnp.ones((), jnp.int32)
    found = (key_rows[lead], value_rows[lead], index * tok_count + lead, last_seg, one)
    everything = jax.tree.map(lambda part: lax.all_gather(part, "seq"), found)
    start = jax.tree.map(jnp.zeros_like, found)

    def lap(k, before):
        new = merge_starts(before, jax.tree.map(lambda part: part[k], everything))
        return jax.tree.map(lambda a, b: jnp.where(k < index, a, b), new, before)

    sink_key, sink_value, sink_pos, sink_seg, sink_has = lax.fori_loop(0, length, lap, start)
    block = jnp.zeros((2 * tok_count, model_width), key_rows.dtype)
    block = block.at[0].set(sink_key).at[tok_count].set(sink_value)
    return (block, jnp.stack([sink_pos, sink_seg, sink_has]))


def table_entry(own, row, entry):
    return own[row : row + 1, entry : entry + 1]


def holder_of(experts, own, pick):
    return sum(
        jnp.where(pick == table_entry(own, OLD_ROW, x), x, 0) for x in range(experts)
    )


def column_routes(experts, routes, own):
    members = len(routes)
    slots = jnp.concatenate([ref[c : c + 1, :] for c in range(2) for ref in routes], axis=0)
    chosen = sum(jnp.where(slots == s, table_entry(own, NEW_ROW, s), 0) for s in range(experts))
    holders = holder_of(experts, own, chosen)
    return tuple((each[:members], each[members:]) for each in (chosen, holders))


def attended(batch, hops, relayed, heads, sinks, bias, own, q, stack, rest, context):
    count = 3 if relayed else hops
    moved, sent, rest = (rest[:count], rest[count : 2 * count], rest[2 * count :])
    if sinks:
        sink_block, sink_info, rest = (rest[0], rest[1], rest[2:])
    tokens, proj = rest
    tok_count, width = tokens.shape[2:]
    window = WIN_BLOCKS * tok_count
    index = lax.axis_index("seq")
    grid = (tok_count, tok_count)

    own_seg = own[batch : batch + 1, :]
    key_segs = [own_seg]
    if relayed:
        pairwise, across, relay = moved
        paired = index % 2 == 1
        key_segs += [jnp.where(paired, sent[0][batch : batch + 1], sent[2][batch : batch + 1])]
        key_segs.append(sent[1][batch : batch + 1, :])
    else:
        key_segs += [ref[batch : batch + 1, :] for ref in sent]
    seg_col = jnp.broadcast_to(own_seg, grid).T
    visible, spans = ([], [])
    for j, key_seg in enumerate(key_segs):
        key_seg = jnp.where(index >= j, key_seg, -1)
        distance = iota(grid, 0) - iota(grid, 1) + tok_count * j
        seen = (seg_col == key_seg) & (distance >= 0) & (distance < window)
        visible.append(jnp.where(seen, 0.0, masked_score))
        low, high = (max(0, tok_count * (j - 1) + 1), min(window, tok_count * (j + 1)) - 1)
        spans.append((distance, low.bit_length(), high.bit_length()))
    if sinks:
        position = index * tok_count + iota(grid, 0)
        seen = (seg_col == sink_info[1]) & (sink_info[2] > 0) & (position - sink_info[0] >= window)
        visible.append(jnp.where(seen & (iota(grid, 1) == 0), 0.0, masked_score))
        spans.append((None, NBUCK - 1, NBUCK - 1))
    lane = iota((tok_count, 128), 1)
    half = width // heads
    keys_at, values_at = (slice(0, tok_count), slice(tok_count, 2 * tok_count))
    for pair in range(heads // 2):
        cols = slice(128 * pair, 128 * pair + 128)
        both = q[batch, 0, :, cols] * score_scale
        even = jnp.where(lane < half, both, jnp.zeros_like(both))
        odd = jnp.where(lane < half, jnp.zeros_like(both), both)
        stacked = jnp.concatenate([even, odd], axis=0)
        blocks = [(stack[keys_at, cols], stack[values_at, cols])]
        if relayed:
            blocks.append(tuple(
                jnp.where(paired, pairwise[at, cols], relay[at, cols])
                for at in (keys_at, values_at)
            ))
            blocks.append((across[keys_at, cols], across[values_at, cols]))
        else:
            for ref in moved:
                blocks.append((ref[keys_at, cols], ref[values_at, cols]))
        if sinks:
            blocks.append((sink_block[keys_at, cols], sink_block[values_at, cols]))
        scores = []
        for (keys, _), (distance, low, high), seen in zip(blocks, spans, visible):
            score = lax.dot_general(stacked, keys, NT, preferred_element_type=f32)
            parts = []
            for side in range(2):
                head = 2 * pair + side
                offset = jnp.full(grid, bias[head, low], f32)
                for bucket in range(low + 1, high + 1):
                    offset = jnp.where(distance >= 1 << (bucket - 1), bias[head, bucket], offset)
                parts.append(score[side * tok_count : (side + 1) * tok_count] + (offset + seen))
            scores.append(jnp.concatenate(parts, axis=0))
        peak = jnp.max(functools.reduce(jnp.maximum, scores), axis=1, keepdims=True)
        weights = [jnp.exp(score - peak) for score in scores]
        total = jnp.sum(functools.reduce(jnp.add, weights), axis=1, keepdims=True)
        scale = 1.0 / total
        mixed = sum(
            jnp.dot((weight * scale).astype(bf16), values, preferred_element_type=f32)
            for weight, (_, values) in zip(weights, blocks)
        )
        context[:, cols] = jnp.where(lane < half, mixed[:tok_count], mixed[tok_count:]).astype(bf16)
    hidden = tokens[batch, 0].astype(f32) + jnp.dot(
        context[...], proj[...], preferred_element_type=f32
    )
    mean = jnp.mean(hidden * hidden, axis=1, keepdims=True)
    return (hidden, (hidden * lax.rsqrt(mean + epsilon)).astype(bf16))


def ranks(member):
    grid = (member.shape[1], member.shape[1])
    earlier = jnp.where(iota(grid, 0) < iota(grid, 1), 1.0, 0.0).astype(bf16)
    return jnp.dot(member.astype(bf16), earlier, preferred_element_type=f32).astype(jnp.int32)


def attend_column_kernel(options, bias, own, q, stack, *rest):
    inputs, (hidden_out, normed_out, context) = (rest[:-3], rest[-3:])
    hidden, normed = attended(1, *options, bias, own, q, stack, inputs, context)
    hidden_out[...] = hidden
    normed_out[...] = normed


def column_places(experts, routes, own):
    me = lax.axis_index("exp")
    _, holders = column_routes(experts, routes, own)
    member = jnp.concatenate(
        [jnp.where((holders[0] == at) | (holders[1] == at), 1.0, 0.0) for at in (me, me ^ 1)],
        axis=0,
    )
    return jnp.where(member > 0.5, ranks(member), -1)


def attend_direct_kernel(options, experts, cap, bias, router_t, own, q, stack, *rest):
    layers = experts // 2
    inputs, rest = (rest[: -4 - layers], rest[-4 - layers :])
    outgoing, (hidden_out, gates_out, rows_out, context) = (rest[:layers], rest[layers:])
    hidden, normed = attended(0, *options, bias, own, q, stack, inputs, context)
    hidden_out[...] = hidden
    tok_count = hidden.shape[0]
    chosen = [own[ONE_ROW + c : ONE_ROW + c + 1, :] for c in range(2)]
    holders = [holder_of(experts, own, pick) for pick in chosen]
    expert = iota((experts, tok_count), 0)
    packet = expert ^ lax.axis_index("exp")
    member = jnp.where((packet == holders[0]) | (packet == holders[1]), 1.0, 0.0)
    place = ranks(member) + expert * cap
    rows = [
        jnp.sum(jnp.where(packet == holder, place, 0), axis=0, keepdims=True) for holder in holders
    ]
    rows_out[...] = jnp.concatenate(rows, axis=0)
    logits = lax.dot_general(router_t[...], normed, NT, preferred_element_type=f32)
    picked = [jnp.sum(jnp.where(expert == c, logits, 0.0), axis=0, keepdims=True) for c in chosen]
    first = jax.nn.sigmoid(picked[0] - picked[1])
    gates_out[...] = jnp.concatenate([first, 1.0 - first], axis=0)
    at = iota((experts * cap, tok_count), 0)
    plan = jnp.where((at == rows[0]) | (at == rows[1]), 1.0, 0.0).astype(bf16)
    packed = jnp.dot(plan, normed, preferred_element_type=f32)
    for m, ref in enumerate(outgoing):
        ref[...] = packed[2 * m * cap : 2 * (m + 1) * cap].astype(bf16)


def picked_rows(members, cap, first_row, places, blocks):
    at = iota((len(members) * cap, blocks[0].shape[0]), 0)
    plans = []
    for n, m in enumerate(members):
        place = places[first_row + m : first_row + m + 1, :]
        place = jnp.where(place >= 0, place + n * cap, -1)
        plans.append(jnp.where(at == place, 1.0, 0.0))
    plan = jnp.concatenate(plans, axis=1).astype(bf16)
    rows = jnp.concatenate([block[...] for block in blocks], axis=0)
    return (jnp.dot(plan, rows, preferred_element_type=f32).astype(bf16), rows)


def pack_kernel(members, cap, columns, places, *rest):
    blocks, out = (rest[:-1], rest[-1])
    out[...], _ = picked_rows(members, cap, columns, places, blocks)


def first_pack_kernel(members, cap, columns, own, *rest):
    routes, blocks, (places, out) = (rest[:columns], rest[columns:-2], rest[-2:])
    places[...] = column_places(2 * columns, routes, own)
    out[...], _ = picked_rows(members, cap, columns, places, blocks)


def numbers_kernel(numbers, own, routes_out, segs_out):
    own[...] = numbers[...]
    routes_out[...] = numbers[TWO_ROW : TWO_ROW + 2, :]
    segs_out[...] = numbers[:2, :]


def collect_kernel(*refs):
    count = len(refs) // 2
    for ref, out in zip(refs[:count], refs[count:]):
        out[...] = ref[...]


def stage_kernel(k, v, q, tokens, out):
    del q, tokens
    tok_count = k.shape[2]
    out[:tok_count, :] = k[0, 0]
    out[tok_count:, :] = v[0, 0]


def join_kernel(k, v, out):
    tok_count = k.shape[0]
    out[:tok_count, :] = k[...]
    out[tok_count:, :] = v[...]


def pass_kernel(*refs):
    del refs


def crossing_kernel(*refs):
    packets, out = (refs[:-1][::-1], refs[-1])
    cap = packets[0].shape[0] // 2
    parts = [ref[...].astype(f32)[cap:] for ref in packets]
    out[...] = jnp.concatenate(parts, axis=0).astype(bf16)


def expert_rows(rows, weights, active, stores):
    gate, up, down = weights
    inner, width = down.shape[1:]
    x = rows[...]
    for begin in range(0, inner, 256):
        span = slice(begin, min(inner, begin + 256))
        gate_part = jnp.dot(x, gate[0, :, span], preferred_element_type=f32)
        up_part = jnp.dot(x, up[0, :, span], preferred_element_type=f32)
        active[:, span] = (jax.nn.gelu(gate_part, approximate=True) * up_part).astype(bf16)
    for begin in range(0, width, 256):
        span = slice(begin, begin + 256)
        part = jnp.dot(active[...], down[0, :, span], preferred_element_type=f32)
        stores(span, part)


def near_kernel(columns, experts, cap, own, places, router_t, *rest):
    blocks, rest = (rest[:columns], rest[columns:])
    routes, rest = (rest[:columns], rest[columns:])
    weights, (out, gates_out, rows, active) = (rest[:3], rest[3:])

    def stores(span, value):
        out[:, span] = value.astype(bf16)

    rows[...], tokens = picked_rows(range(columns), cap, 0, places, blocks)
    logits = lax.dot_general(router_t[...], tokens, NT, preferred_element_type=f32)
    chosen, holders = column_routes(experts, routes, own)
    chosen = [
        jnp.concatenate([picks[m : m + 1, :] for m in range(columns)], axis=1) for picks in chosen
    ]
    expert = iota(logits.shape, 0)
    picked = [
        jnp.sum(jnp.where(expert == pick, logits, 0.0), axis=0, keepdims=True) for pick in chosen
    ]
    first = jax.nn.sigmoid(picked[0] - picked[1])
    tok_count = places.shape[1]
    first = jnp.concatenate(
        [first[:, m * tok_count : (m + 1) * tok_count] for m in range(columns)], axis=0
    )
    me = lax.axis_index("exp")
    gates_out[...] = jnp.concatenate(
        [
            jnp.where(holders[0] == at, first, 0.0) + jnp.where(holders[1] == at, 1.0 - first, 0.0)
            for at in (me, me ^ 1)
        ],
        axis=0,
    )
    expert_rows(rows, weights, active, stores)


def far_kernel(low_in, high_in, *rest):
    weights, (low_out, high_out, rows, active) = (rest[:3], rest[3:])
    part = low_in.shape[0]

    def stores(span, value):
        low_out[:, span] = value[:part].astype(bf16)
        high_out[:, span] = value[part:].astype(bf16)

    rows[:part, :] = low_in[...]
    rows[part:, :] = high_in[...]
    expert_rows(rows, weights, active, stores)


def direct_kernel(layers, *refs):
    packets, crossed, weights = (refs[:layers][::-1], refs[layers], refs[layers + 1 : layers + 4])
    near, far, rows, active = refs[layers + 4 :]
    cap = packets[0].shape[0] // 2
    half = layers * cap

    def stores(span, value):
        near[:, span] = value[:half].astype(bf16)
        far[:, span] = value[half:].astype(bf16)

    parts = [ref[...].astype(f32)[:cap] for ref in packets]
    rows[:half, :] = jnp.concatenate(parts, axis=0).astype(bf16)
    rows[half:, :] = crossed[...]
    expert_rows(rows, weights, active, stores)


def rejoin_kernel(near, far, *outs):
    cap = outs[0].shape[0] // 2
    both = [ref[...].astype(f32) for ref in (near, far)]
    for m, out in enumerate(outs):
        parts = [each[m * cap : (m + 1) * cap] for each in both]
        out[...] = jnp.concatenate(parts, axis=0).astype(bf16)


def partial_kernel(members, cap, columns, places, gates, near, far, *outs):
    at = iota((cap, places.shape[1]), 0)
    for n, m in enumerate(members):
        total = None
        near_rows = near[m * cap : (m + 1) * cap, :]
        far_rows = far[n * cap : (n + 1) * cap, :]
        for values, row in ((near_rows, m), (far_rows, columns + m)):
            spread = jnp.where(at == places[row : row + 1, :], gates[row : row + 1, :], 0.0)
            coarse = spread.astype(bf16)
            fine = (spread - coarse.astype(f32)).astype(bf16)
            for half in (coarse, fine):
                term = lax.dot_general(half, values, TN, preferred_element_type=f32)
                total = term if total is None else total + term
        outs[n][...] = total.astype(outs[n].dtype)


def fold_kernel(own, *rest):
    total = own[...]
    for ref in rest[:-1]:
        total = total + ref[...].astype(f32)
    rest[-1][...] = total.astype(rest[-1].dtype)


def final_kernel(layers, hidden, gates, rows, *rest):
    packets, ends, out = (rest[:layers][::-1], rest[layers:-1], rest[-1])
    at = iota((layers * packets[0].shape[0], hidden.shape[0]), 0)
    spread = jnp.where(at == rows[0:1, :], gates[0:1, :], 0.0)
    spread = spread + jnp.where(at == rows[1:2, :], gates[1:2, :], 0.0)
    coarse = spread.astype(bf16)
    fine = (spread - coarse.astype(f32)).astype(bf16)
    values = jnp.concatenate([ref[...].astype(f32) for ref in packets], axis=0).astype(bf16)
    total = hidden[...]
    for half in (coarse, fine):
        total = total + lax.dot_general(half, values, TN, preferred_element_type=f32)
    out[0, 0] = total.astype(bf16)
    total = ends[0][...]
    for ref in ends[1:]:
        total = total + ref[...].astype(f32)
    out[1, 0] = total.astype(bf16)


def local(
    tokens, queries, key_rows, value_rows, segments, bias_table, out_proj, router,
    gate_weight, up_weight, down_weight, old_table, new_table, routes_one, routes_two,
):
    tok_count, width = tokens.shape[2:]
    heads = bias_table.shape[0]
    experts = router.shape[1]
    columns = experts // 2
    inner = gate_weight.shape[2]
    seq_size = lax.axis_size("seq")
    seq_len = tok_count * seq_size
    capacity = tok_count * 2 * 5 // (4 * experts)
    longest = seq_len // 2
    hops = min(WIN_BLOCKS, (longest - 1 + tok_count - 1) // tok_count)
    relayed = seq_size == 4 and hops == 2
    sinks = seq_len > WIN_BLOCKS * tok_count
    weights = (gate_weight, up_weight, down_weight)
    router_t = router.T
    lower, upper = (range(columns // 2), range(columns // 2, columns))
    rows_bf16 = shaped((tok_count, width), bf16)
    rows_f32 = shaped((tok_count, width), f32)
    cap_two = capacity * MAX_SLOTS
    slots = columns * cap_two
    part_two = slots // 2
    packet = shaped((2 * capacity, width), bf16)
    stack_shape = shaped((2 * tok_count, width), bf16)
    latest = []

    def call(kernel, outs, ins, args, scratch=(), after=(), aliases=None, work=1):
        after = [*after, *latest]
        out_specs = jax.tree.map(lambda _: VMEM, outs)
        if aliases:
            out_specs = tuple(ANY if n in aliases.values() else VMEM for n in range(len(outs)))

        def body(*refs):
            kernel(*refs[: len(args)], *refs[len(args) + len(after) :])

        made = pl.pallas_call(
            body,
            out_shape=outs,
            in_specs=ins + [ANY] * len(after),
            out_specs=out_specs,
            scratch_shapes=list(scratch),
            input_output_aliases=aliases or {},
            compiler_params=pltpu.CompilerParams(vmem_limit_bytes=24 * 2**20),
            cost_estimate=pl.CostEstimate(flops=work, bytes_accessed=1, transcendentals=0),
        )(*args, *after)
        latest[:] = jax.tree.leaves(made)[:1]
        return made

    def multicast(own):
        blocks = {0: own}
        bit = columns // 2
        while bit:
            for m in sorted(blocks):
                blocks[m | bit] = swapped(blocks[m], "exp", 2 * bit)
            bit //= 2
        return blocks

    def chained(moving):
        moved = []
        for _ in range(hops):
            moving = passed_along(moving, "seq", 1)
            moved.append(moving)
        return moved

    def options(batch):
        extra = []
        if sinks:
            extra = latest_start(key_rows[batch, 0], value_rows[batch, 0], segments[batch, 0])
        return ((hops, relayed, heads, sinks), extra)

    def attend_column(moved):
        settings, extra = options(1)
        return call(
            functools.partial(attend_column_kernel, settings),
            (rows_f32, rows_bf16),
            [SMEM] + [VMEM] * (3 + 2 * len(moved)) + ([VMEM, SMEM] if sinks else [])
            + [VMEM] * 2,
            (bias_table, own, queries, stacks[1], *moved, *sent, *extra, tokens, out_proj),
            scratch=[pltpu.VMEM((tok_count, width), bf16)],
        )

    def attend_direct(moved):
        settings, extra = options(0)
        return call(
            functools.partial(attend_direct_kernel, settings, experts, capacity),
            (*[packet] * columns, rows_f32, shaped((2, tok_count), f32),
             shaped((2, tok_count), jnp.int32)),
            [SMEM] + [VMEM] * (4 + 2 * len(moved)) + ([VMEM, SMEM] if sinks else [])
            + [VMEM] * 2,
            (bias_table, router_t, own, queries, stacks[0], *moved, *sent, *extra, tokens,
             out_proj),
            scratch=[pltpu.VMEM((tok_count, width), bf16)],
        )

    def scratch_for(slots):
        return (pltpu.VMEM((slots, width), bf16), pltpu.VMEM((slots, inner), bf16))

    def pack(members, places, blocks):
        return call(
            functools.partial(pack_kernel, members, cap_two, columns),
            shaped((part_two, width), bf16),
            [VMEM] * (1 + len(members)),
            (places, *(blocks[m] for m in members)),
        )

    def partial(members, far):
        parts = call(
            functools.partial(partial_kernel, members, cap_two, columns),
            tuple(rows_bf16 if m % 2 else rows_f32 for m in members),
            [VMEM] * 4,
            (places, gates_two, near, far),
        )
        for m, value in zip(members, parts):
            totals.setdefault(m, []).insert(0, value)

    def send_down(members):
        for m in sorted(members, key=lambda m: (m & -m, -m)):
            parts = totals[m]
            value = parts[0]
            if len(parts) > 1:
                value = call(
                    fold_kernel, rows_bf16, [VMEM] * len(parts), parts, work=6 * 10**9
                )
            totals.setdefault(m & (m - 1), []).append(swapped(value, "exp", 2 * (m & -m)))

    stacked = call(join_kernel, stack_shape, [VMEM] * 2, (key_rows[1, 0], value_rows[1, 0]))
    first_hop = swapped(stacked, "seq", 1) if relayed else passed_along(stacked, "seq", 1)
    tables = [jnp.pad(table, (0, tok_count - experts))[None] for table in (new_table, old_table)]
    numbers = jnp.concatenate([segments[:, 0], routes_one[0].T, routes_two[0].T, *tables])
    own, own_routes, own_segs = call(
        numbers_kernel,
        tuple(shaped((rows, tok_count), jnp.int32) for rows in (8, 2, 2)),
        [VMEM], (numbers,), after=[first_hop],
    )
    routes = multicast(own_routes)
    if relayed:
        sent = [swapped(own_segs, "seq", mask) for mask in (1, 2, 3)]
        across = swapped(stacked, "seq", 2)
    else:
        sent = chained(own_segs)
        across = first_hop
    stack_one = call(
        stage_kernel, stack_shape, [VMEM] * 4, (key_rows, value_rows, queries, tokens),
        after=[routes[columns // 2]],
    )
    *routes, latest_seg = call(
        collect_kernel,
        tuple(shaped((2, tok_count), jnp.int32) for _ in range(columns + 1)),
        [VMEM] * (columns + 1),
        (*(routes[m] for m in range(columns)), sent[-1]),
        after=sent[:-1],
    )
    sent = [*sent[:-1], latest_seg]
    (across,) = call(pass_kernel, (stack_shape,), [ANY], (across,), aliases={0: 0})
    if relayed:
        moved_two = [first_hop, across, swapped(across, "seq", 1)]
    else:
        moved_two = [across]
        while len(moved_two) < hops:
            moved_two.append(passed_along(moved_two[-1], "seq", 1))
    stacks = [stack_one, stacked]
    hidden_two, normed_two = attend_column(moved_two)
    (stack_one,) = call(
        pass_kernel, (stack_shape,), [ANY], (stack_one,), aliases={0: 0}
    )
    stacks[0] = stack_one
    if relayed:
        moved_one = [
            swapped(stack_one, "seq", 1),
            swapped(stack_one, "seq", 2),
            lax.ppermute(stack_one, "seq", [(0, 0), (1, 2), (2, 1), (3, 3)]),
        ]
    else:
        moved_one = chained(stack_one)
    blocks = multicast(normed_two)
    places, low_in = call(
        functools.partial(first_pack_kernel, lower, cap_two, columns),
        (shaped((2 * columns, tok_count), jnp.int32), shaped((part_two, width), bf16)),
        [VMEM] * (1 + columns + len(lower)),
        (own, *routes, *(blocks[m] for m in lower)), work=4 * 10**9,
    )
    low_in = swapped(low_in, "exp", 1)
    high_in = swapped(pack(upper, places, blocks), "exp", 1)
    *packets, hidden_one, gates_one, rows_one = attend_direct(moved_one)
    arrived = [packets[0]] + [swapped(packets[m], "exp", 2 * m) for m in range(1, columns)]
    low_out, high_out = call(
        far_kernel,
        (shaped((part_two, width), bf16),) * 2,
        [VMEM] * 5,
        (low_in, high_in, *weights),
        scratch=scratch_for(slots),
    )
    high_far = swapped(high_out, "exp", 1)
    near, gates_two = call(
        functools.partial(near_kernel, columns, experts, cap_two),
        (shaped((slots, width), bf16), shaped((2 * columns, tok_count), f32)),
        [VMEM] * (6 + 2 * columns),
        (own, places, router_t, *(blocks[m] for m in range(columns)), *routes, *weights),
        scratch=scratch_for(slots), work=4 * 10**9,
    )
    crossing = call(
        crossing_kernel, shaped((columns * capacity, width), bf16), [VMEM] * columns, arrived[::-1],
        work=2 * 10**10,
    )
    crossed_one = swapped(crossing, "exp", 1)
    totals = {}
    partial(upper, high_far)
    send_down(m for m in upper if m % 2)
    (low_out,) = call(
        pass_kernel, (shaped(low_out.shape, bf16),), [ANY], (low_out,), aliases={0: 0},
        after=[crossed_one],
    )
    low_far = swapped(low_out, "exp", 1)
    near_one, far_one = call(
        functools.partial(direct_kernel, columns),
        (shaped((columns * capacity, width), bf16),) * 2,
        [VMEM] * (4 + columns),
        (*arrived[::-1], crossed_one, *weights),
        scratch=scratch_for(experts * capacity),
    )
    far_one = swapped(far_one, "exp", 1)
    send_down(m for m in upper if m % 2 == 0)
    partial(lower, low_far)
    send_down(m for m in lower if m)
    answers = call(rejoin_kernel, [packet] * columns, [VMEM] * 2, (near_one, far_one))
    returned = [answers[0]] + [swapped(answers[m], "exp", 2 * m) for m in range(1, columns)]
    far_part, rest = (totals[0][1], [hidden_two, totals[0][0], *totals[0][2:]])
    ends = (call(fold_kernel, rows_f32, [VMEM] * 2, (rest[0], far_part)), *rest[1:])
    return call(
        functools.partial(final_kernel, columns), shaped((2, 1, tok_count, width), bf16),
        [VMEM] * (3 + columns + len(ends)), (hidden_one, gates_one, rows_one, *returned[::-1], *ends),
    )


def solution(mesh):
    rows = P(None, "exp", "seq", None)
    placed = (
        rows, rows, rows, rows, P(None, "exp", "seq"), P(), P(), P(),
        P("exp", None, None), P("exp", None, None), P("exp", None, None), P(), P(),
        P("exp", "seq", None), P("exp", "seq", None),
    )
    return jax.shard_map(local, mesh=mesh, in_specs=placed, out_specs=rows, check_vma=False)
```

profile of v0, /device:TPU:0, one launch (start us, length us, event | category | flops | bytes accessed | tf_op | source)
XLA Modules:
  0.0 109.5 jit_solution(2859606504775770702)
XLA Ops:
  0.0 1.2 %slice_bitcast_fusion = (bf16[128,1024]{1,0:T(8,128)(2,1)S(1)}, bf16[128,1024]{1,0:T(8,128)(2,1)S(1)}) fusion(bf16[2,1,128,1024]{3,2,1,0:T(8,128)(2,1)} %refs_1_.1, bf16[2,1,128,1024]{3,2,1,0:T(8,128)(2,1)} %refs_0_.3), kind=kLoop, calls=%fused_computation | loop fusion | bytes 1048576 | tf_op jit(solution)/shard_map/squeeze | solution.py:535
  1.2 0.0 copy-start.8
  1.2 0.8 shard_map.145.refs_2_.refs_3_
  2.0 0.5 collective-permute-start
  2.5 2.5 %collective-permute-start.2 = (bf16[256,1024]{1,0:T(8,128)(2,1)}, bf16[256,1024]{1,0:T(8,128)(2,1)}, u32[]{:S(2)}, u32[]{:S(2)}) collective-permute-start(bf16[256,1024]{1,0:T(8,128)(2,1)} %shard_map.145.refs_2_.refs_3_), channel_id=1, source_target_pairs={{0,16},{8,24},{16,0},{24,8},{1,17},{9,25},{17,1},{25,9},{2,18},{10... | collective-permute-start | bytes 1572872 | tf_op jit(solution)/shard_map/ppermute | solution.py:43
  4.9 0.7 pad_bitcast_fusion
  5.6 0.7 concatenate.3.refs_0_
  6.4 2.7 %collective-permute-start.1 = (s32[2,128]{1,0:T(2,128)S(1)}, s32[2,128]{1,0:T(2,128)S(1)}, u32[]{:S(2)}, u32[]{:S(2)}) collective-permute-start(s32[2,128]{1,0:T(2,128)S(1)} %get-tuple-element.39.refs_0_), channel_id=1, source_target_pairs={{0,4},{1,5},{2,6},{3,7},{4,0},{5,1},{6,2},{7,3},{8,12},{9,13},{10,... | collective-permute-start | bytes 3080 | tf_op jit(solution)/shard_map/ppermute | solution.py:43
  9.0 0.0 collective-permute-start.6
  9.0 0.8 collective-permute-start.7
  9.8 1.6 %collective-permute-start.3 = (s32[2,128]{1,0:T(2,128)S(1)}, s32[2,128]{1,0:T(2,128)S(1)}, u32[]{:S(2)}, u32[]{:S(2)}) collective-permute-start(s32[2,128]{1,0:T(2,128)S(1)} %get-tuple-element.39.refs_0_), channel_id=1, source_target_pairs={{0,2},{1,3},{2,0},{3,1},{4,6},{5,7},{6,4},{7,5},{8,10},{9,11},{10,... | collective-permute-start | bytes 3080 | tf_op jit(solution)/shard_map/ppermute | solution.py:43
  11.4 0.8 collective-permute-start.5
  12.2 0.5 collective-permute-start.4
  12.6 1.0 copy-done.6
  13.7 1.0 copy-done.7
  14.8 3.1 %collective-permute-done.7.refs_6_.refs_8_.refs_9_ = s32[2,128]{1,0:T(2,128)S(1)} collective-permute-done((s32[2,128]{1,0:T(2,128)S(1)}, s32[2,128]{1,0:T(2,128)S(1)}, u32[]{:S(2)}, u32[]{:S(2)}) %collective-permute-start.7) | collective-permute-done | bytes 1056 | tf_op jit(solution)/shard_map/ppermute | solution.py:43
  17.9 0.0 collective-permute-done.5.refs_4_
  17.9 0.0 collective-permute-done.4.refs_3_
  17.9 0.2 collective-permute-start.8
  18.1 2.0 %collective-permute-done.8.refs_6_ = bf16[256,1024]{1,0:T(8,128)(2,1)S(1)} collective-permute-done((bf16[256,1024]{1,0:T(8,128)(2,1)}, bf16[256,1024]{1,0:T(8,128)(2,1)S(1)}, u32[]{:S(2)}, u32[]{:S(2)}) %collective-permute-start.8) | collective-permute-done | bytes 524320 | tf_op jit(solution)/shard_map/ppermute | solution.py:43
  20.1 4.0 %shard_map.150 = (f32[128,1024]{1,0:T(8,128)S(1)}, bf16[128,1024]{1,0:T(8,128)(2,1)S(1)}) custom-call(f32[16,32]{1,0:T(8,128)S(1)} %copy-done.8, s32[8,128]{1,0:T(8,128)S(1)} %get-tuple-element.38.refs_5_.refs_1_.refs_0_.refs_2_, bf16[2,1,128,1024]{3,2,1,0:T(8,128)(2,1)S(1)} %copy-done.4, bf16[256,1024]{1,0:T(8,128)(2,1)} %shard_map.145.refs_2_.refs_3_, ...), custom_call_target="tpu_custom_call" | custom-call | flops 1 | bytes 1 | tf_op jit(solution)/shard_map/pallas_call | solution.py:445
  24.1 2.9 %collective-permute-start.13 = (bf16[128,1024]{1,0:T(8,128)(2,1)S(1)}, bf16[128,1024]{1,0:T(8,128)(2,1)S(1)}, u32[]{:S(2)}, u32[]{:S(2)}) collective-permute-start(bf16[128,1024]{1,0:T(8,128)(2,1)S(1)} %get-tuple-element.47.refs_5_.refs_3_), channel_id=1, source_target_pairs={{0,4},{1,5},{2,6},{3,7},{4,0},{5,1},{6,2},{7,3},{8,12},{9,13},{10,... | collective-permute-start | bytes 786440 | tf_op jit(solution)/shard_map/ppermute | solution.py:43
  27.0 1.6 %collective-permute-start.12 = (bf16[128,1024]{1,0:T(8,128)(2,1)S(1)}, bf16[128,1024]{1,0:T(8,128)(2,1)S(1)}, u32[]{:S(2)}, u32[]{:S(2)}) collective-permute-start(bf16[128,1024]{1,0:T(8,128)(2,1)S(1)} %get-tuple-element.47.refs_5_.refs_3_), channel_id=1, source_target_pairs={{0,2},{1,3},{2,0},{3,1},{4,6},{5,7},{6,4},{7,5},{8,10},{9,11},{10,... | collective-permute-start | bytes 786440 | tf_op jit(solution)/shard_map/ppermute | solution.py:43
  28.6 1.5 %collective-permute-start.10 = (bf16[256,1024]{1,0:T(8,128)(2,1)S(1)}, bf16[256,1024]{1,0:T(8,128)(2,1)S(1)}, u32[]{:S(2)}, u32[]{:S(2)}) collective-permute-start(bf16[256,1024]{1,0:T(8,128)(2,1)S(1)} %shard_map.151.refs_7_.refs_4_), channel_id=1, source_target_pairs={{0,16},{8,24},{16,0},{24,8},{1,17},{9,25},{17,1},{25,9},{2,18},{10... | collective-permute-start | bytes 1572872 | tf_op jit(solution)/shard_map/ppermute | solution.py:43
  30.1 0.9 collective-permute-start.11
  30.9 1.9 %collective-permute-start.9 = (bf16[256,1024]{1,0:T(8,128)(2,1)S(1)}, bf16[256,1024]{1,0:T(8,128)(2,1)S(1)}, u32[]{:S(2)}, u32[]{:S(2)}) collective-permute-start(bf16[256,1024]{1,0:T(8,128)(2,1)S(1)} %shard_map.151.refs_7_.refs_4_), channel_id=1, source_target_pairs={{0,8},{8,0},{16,24},{24,16},{1,9},{9,1},{17,25},{25,17},{2,10},{10... | collective-permute-start | bytes 1572872 | tf_op jit(solution)/shard_map/ppermute | solution.py:43
  32.9 6.5 %collective-permute-done.13.refs_1_.refs_5_ = bf16[128,1024]{1,0:T(8,128)(2,1)S(1)} collective-permute-done((bf16[128,1024]{1,0:T(8,128)(2,1)S(1)}, bf16[128,1024]{1,0:T(8,128)(2,1)S(1)}, u32[]{:S(2)}, u32[]{:S(2)}) %collective-permute-start.13) | collective-permute-done | bytes 262176 | tf_op jit(solution)/shard_map/ppermute | solution.py:43
  39.3 0.6 collective-permute-start.14
  39.9 0.5 shard_map.152
  40.4 1.6 %collective-permute-start.18 = (bf16[160,1024]{1,0:T(8,128)(2,1)S(1)}, bf16[160,1024]{1,0:T(8,128)(2,1)S(1)}, u32[]{:S(2)}, u32[]{:S(2)}) collective-permute-start(bf16[160,1024]{1,0:T(8,128)(2,1)S(1)} %get-tuple-element.56), channel_id=1, source_target_pairs={{0,1},{1,0},{2,3},{3,2},{4,5},{5,4},{6,7},{7,6},{8,9},{9,8},{10,11... | collective-permute-start | bytes 983048 | tf_op jit(solution)/shard_map/ppermute | solution.py:43
  42.0 5.0 %collective-permute-done.14.refs_2_.refs_6_ = bf16[128,1024]{1,0:T(8,128)(2,1)S(1)} collective-permute-done((bf16[128,1024]{1,0:T(8,128)(2,1)S(1)}, bf16[128,1024]{1,0:T(8,128)(2,1)S(1)}, u32[]{:S(2)}, u32[]{:S(2)}) %collective-permute-start.14) | collective-permute-done | bytes 262176 | tf_op jit(solution)/shard_map/ppermute | solution.py:43
  47.0 0.2 shard_map.153.refs_13_
  47.3 0.0 copy-start
  47.3 1.4 %collective-permute-start.19 = (bf16[160,1024]{1,0:T(8,128)(2,1)S(1)}, bf16[160,1024]{1,0:T(8,128)(2,1)S(1)}, u32[]{:S(2)}, u32[]{:S(2)}) collective-permute-start(bf16[160,1024]{1,0:T(8,128)(2,1)S(1)} %shard_map.153.refs_13_), channel_id=1, source_target_pairs={{0,1},{1,0},{2,3},{3,2},{4,5},{5,4},{6,7},{7,6},{8,9},{9,8},{10,11... | collective-permute-start | bytes 983048 | tf_op jit(solution)/shard_map/ppermute | solution.py:43
  48.7 0.0 collective-permute-done.11.refs_7_
  48.7 0.0 collective-permute-done.9.refs_5_
  48.7 3.7 %shard_map.154 = (bf16[80,1024]{1,0:T(8,128)(2,1)S(1)}, bf16[80,1024]{1,0:T(8,128)(2,1)S(1)}, bf16[80,1024]{1,0:T(8,128)(2,1)S(1)}, bf16[80,1024]{1,0:T(8,128)(2...) custom-call(f32[16,32]{1,0:T(8,128)S(1)} %copy-done.8, ...), custom_call_target="tpu_custom_call" | custom-call | flops 1 | bytes 1 | tf_op jit(solution)/shard_map/pallas_call | solution.py:445
  52.4 4.2 %collective-permute-start.15 = (bf16[80,1024]{1,0:T(8,128)(2,1)S(1)}, bf16[80,1024]{1,0:T(8,128)(2,1)S(1)}, u32[]{:S(2)}, u32[]{:S(2)}) collective-permute-start(bf16[80,1024]{1,0:T(8,128)(2,1)S(1)} %get-tuple-element.52), channel_id=1, source_target_pairs={{0,6},{1,7},{2,4},{3,5},{4,2},{5,3},{6,0},{7,1},{8,14},{9,15},{10,... | collective-permute-start | bytes 491528 | tf_op jit(solution)/shard_map/ppermute | solution.py:43
  56.6 0.0 collective-permute-start.16
  56.6 0.6 collective-permute-start.17
  57.3 0.0 collective-permute-done.18.refs_0_
  57.3 3.3 %shard_map.155 = (bf16[160,1024]{1,0:T(8,128)(2,1)S(1)}, bf16[160,1024]{1,0:T(8,128)(2,1)S(1)}) custom-call(bf16[160,1024]{1,0:T(8,128)(2,1)S(1)} %collective-permute-done.18.refs_0_, bf16[160,1024]{1,0:T(8,128)(2,1)S(1)} %collective-permute-done.19.refs_1_, bf16[1,1024,1408]{2,1,0:T(8,128)(2,1)S(1)} %copy-done, bf16[1,1024,1408]{2,1,0:T(8,128)(2,1)S(1)} %copy-done.1, ...), custom_call_target="tpu_custom_call" | custom-call | flops 1 | bytes 1 | tf_op jit(solution)/shard_map/pallas_call | solution.py:445
  60.6 1.2 %collective-permute-start.21 = (bf16[160,1024]{1,0:T(8,128)(2,1)S(1)}, bf16[160,1024]{1,0:T(8,128)(2,1)S(1)}, u32[]{:S(2)}, u32[]{:S(2)}) collective-permute-start(bf16[160,1024]{1,0:T(8,128)(2,1)S(1)} %get-tuple-element.60), channel_id=1, source_target_pairs={{0,1},{1,0},{2,3},{3,2},{4,5},{5,4},{6,7},{7,6},{8,9},{9,8},{10,11... | collective-permute-start | bytes 983048 | tf_op jit(solution)/shard_map/ppermute | solution.py:43
  61.8 3.9 %shard_map.156 = (bf16[320,1024]{1,0:T(8,128)(2,1)S(1)}, f32[8,128]{1,0:T(8,128)S(1)}) custom-call(s32[8,128]{1,0:T(8,128)S(1)} %get-tuple-element.38.refs_5_.refs_1_.refs_0_.refs_2_, s32[8,128]{1,0:T(8,128)S(1)} %get-tuple-element.48.refs_0_.refs_3_.refs_1_, bf16[8,1024]{1,0:T(8,128)(2,1)S(1)} %bitcast.17, ...), custom_call_target="tpu_custom_call" | custom-call | flops 4000000000 | bytes 1 | tf_op jit(solution)/shard_map/pallas_call | solution.py:445
  65.7 3.9 %collective-permute-done.16.refs_1_ = bf16[80,1024]{1,0:T(8,128)(2,1)S(1)} collective-permute-done((bf16[80,1024]{1,0:T(8,128)(2,1)S(1)}, bf16[80,1024]{1,0:T(8,128)(2,1)S(1)}, u32[]{:S(2)}, u32[]{:S(2)}) %collective-permute-start.16) | collective-permute-done | bytes 163872 | tf_op jit(solution)/shard_map/ppermute | solution.py:43
  69.6 0.6 collective-permute-start.20
  70.2 0.7 shard_map.158
  70.9 0.1 collective-permute-start.24
  71.0 7.4 %collective-permute-done.20.refs_1_.refs_4_ = bf16[160,1024]{1,0:T(8,128)(2,1)S(1)} collective-permute-done((bf16[160,1024]{1,0:T(8,128)(2,1)S(1)}, bf16[160,1024]{1,0:T(8,128)(2,1)S(1)}, u32[]{:S(2)}, u32[]{:S(2)}) %collective-permute-start.20) | collective-permute-done | bytes 327712 | tf_op jit(solution)/shard_map/ppermute | solution.py:43
  78.4 0.3 collective-permute-start.23
  78.7 3.3 %shard_map.160 = (bf16[160,1024]{1,0:T(8,128)(2,1)S(1)}, bf16[160,1024]{1,0:T(8,128)(2,1)S(1)}) custom-call(bf16[80,1024]{1,0:T(8,128)(2,1)S(1)} %collective-permute-done.15.refs_0_, bf16[80,1024]{1,0:T(8,128)(2,1)S(1)} %collective-permute-done.16.refs_1_, bf16[80,1024]{1,0:T(8,128)(2,1)S(1)} %collective-permute-done.17.refs_2_, ...), custom_call_target="tpu_custom_call" | custom-call | flops 1 | bytes 1 | tf_op jit(solution)/shard_map/pallas_call | solution.py:445
  82.0 1.8 %collective-permute-start.22 = (bf16[160,1024]{1,0:T(8,128)(2,1)S(1)}, bf16[160,1024]{1,0:T(8,128)(2,1)S(1)}, u32[]{:S(2)}, u32[]{:S(2)}) collective-permute-start(bf16[160,1024]{1,0:T(8,128)(2,1)S(1)} %get-tuple-element.63), channel_id=1, source_target_pairs={{0,1},{1,0},{2,3},{3,2},{4,5},{5,4},{6,7},{7,6},{8,9},{9,8},{10,11... | collective-permute-start | bytes 983048 | tf_op jit(solution)/shard_map/ppermute | solution.py:43
  83.8 0.1 shard_map.161.refs_4_
  83.9 1.2 %collective-permute-start.28 = (bf16[128,1024]{1,0:T(8,128)(2,1)S(1)}, bf16[128,1024]{1,0:T(8,128)(2,1)S(1)}, u32[]{:S(2)}, u32[]{:S(2)}) collective-permute-start(bf16[128,1024]{1,0:T(8,128)(2,1)S(1)} %shard_map.161.refs_4_), channel_id=1, source_target_pairs={{0,4},{1,5},{2,6},{3,7},{4,0},{5,1},{6,2},{7,3},{8,12},{9,13},{10,... | collective-permute-start | bytes 786440 | tf_op jit(solution)/shard_map/ppermute | solution.py:43
  85.0 4.0 %collective-permute-done.23.refs_3_ = bf16[160,1024]{1,0:T(8,128)(2,1)S(1)} collective-permute-done((bf16[160,1024]{1,0:T(8,128)(2,1)S(1)}, bf16[160,1024]{1,0:T(8,128)(2,1)S(1)}, u32[]{:S(2)}, u32[]{:S(2)}) %collective-permute-start.23) | collective-permute-done | bytes 327712 | tf_op jit(solution)/shard_map/ppermute | solution.py:43
  89.0 0.7 shard_map.162
  89.8 0.1 collective-permute-start.29
  89.8 3.3 %collective-permute-done.22.refs_1_ = bf16[160,1024]{1,0:T(8,128)(2,1)S(1)} collective-permute-done((bf16[160,1024]{1,0:T(8,128)(2,1)S(1)}, bf16[160,1024]{1,0:T(8,128)(2,1)S(1)}, u32[]{:S(2)}, u32[]{:S(2)}) %collective-permute-start.22) | collective-permute-done | bytes 327712 | tf_op jit(solution)/shard_map/ppermute | solution.py:43
  93.2 0.9 collective-permute-start.25
  94.1 0.8 collective-permute-start.26
  94.9 2.8 %collective-permute-start.27 = (bf16[80,1024]{1,0:T(8,128)(2,1)S(1)}, bf16[80,1024]{1,0:T(8,128)(2,1)S(1)}, u32[]{:S(2)}, u32[]{:S(2)}) collective-permute-start(bf16[80,1024]{1,0:T(8,128)(2,1)S(1)} %get-tuple-element.68), channel_id=1, source_target_pairs={{0,2},{1,3},{2,0},{3,1},{4,6},{5,7},{6,4},{7,5},{8,10},{9,11},{10,... | collective-permute-start | bytes 491528 | tf_op jit(solution)/shard_map/ppermute | solution.py:43
  97.7 4.5 %collective-permute-done.25.refs_3_ = bf16[80,1024]{1,0:T(8,128)(2,1)S(1)} collective-permute-done((bf16[80,1024]{1,0:T(8,128)(2,1)S(1)}, bf16[80,1024]{1,0:T(8,128)(2,1)S(1)}, u32[]{:S(2)}, u32[]{:S(2)}) %collective-permute-start.25) | collective-permute-done | bytes 163872 | tf_op jit(solution)/shard_map/ppermute | solution.py:43
  102.3 5.9 %collective-permute-done.26.refs_4_ = bf16[80,1024]{1,0:T(8,128)(2,1)S(1)} collective-permute-done((bf16[80,1024]{1,0:T(8,128)(2,1)S(1)}, bf16[80,1024]{1,0:T(8,128)(2,1)S(1)}, u32[]{:S(2)}, u32[]{:S(2)}) %collective-permute-start.26) | collective-permute-done | bytes 163872 | tf_op jit(solution)/shard_map/ppermute | solution.py:43
  108.2 1.4 %shard_map.165 = bf16[2,1,128,1024]{3,2,1,0:T(8,128)(2,1)} custom-call(f32[128,1024]{1,0:T(8,128)S(1)} %get-tuple-element.49.refs_0_, f32[2,128]{1,0:T(2,128)S(1)} %get-tuple-element.50.refs_1_, s32[2,128]{1,0:T(2,128)S(1)} %get-tuple-element.51.refs_2_, bf16[80,1024]{1,0:T(8,128)(2,1)S(1)} %collective-permute-done.25.refs_3_, ...), custom_call_target="tpu_custom_call" | custom-call | flops 1 | bytes 1 | tf_op jit(solution)/shard_map/pallas_call | solution.py:445
  (40 shorter events, 0.2 us)
Async XLA Ops:
  0.0 12.6 %copy-start.5 = (bf16[2,1,128,1024]{3,2,1,0:T(8,128)(2,1)S(1)}, bf16[2,1,128,1024]{3,2,1,0:T(8,128)(2,1)}, u32[]{:S(2)}) copy-start(bf16[2,1,128,1024]{3,2,1,0:T(8,128)(2,1)} %refs_11_.4) | copy-start | bytes 1572868
  0.0 12.6 %copy-start.4 = (bf16[2,1,128,1024]{3,2,1,0:T(8,128)(2,1)S(1)}, bf16[2,1,128,1024]{3,2,1,0:T(8,128)(2,1)}, u32[]{:S(2)}) copy-start(bf16[2,1,128,1024]{3,2,1,0:T(8,128)(2,1)} %refs_3_.4) | copy-start | bytes 1572868
  1.2 19.0 %copy-start.8 = (f32[16,32]{1,0:T(8,128)S(1)}, f32[16,32]{1,0:T(8,128)}, u32[]{:S(2)}) copy-start(f32[16,32]{1,0:T(8,128)} %refs_0_.5) | copy-start | bytes 6148
  2.0 18.1 %copy-start.3 = (bf16[1024,1024]{1,0:T(8,128)(2,1)S(1)}, bf16[1024,1024]{1,0:T(8,128)(2,1)}, u32[]{:S(2)}) copy-start(bf16[1024,1024]{1,0:T(8,128)(2,1)} %refs_12_.2) | copy-start | bytes 6291460
  2.0 4.3 %collective-permute-start = (bf16[256,1024]{1,0:T(8,128)(2,1)}, bf16[256,1024]{1,0:T(8,128)(2,1)}, u32[]{:S(2)}, u32[]{:S(2)}) collective-permute-start(bf16[256,1024]{1,0:T(8,128)(2,1)} %shard_map.145.refs_2_.refs_3_), channel_id=1, source_target_pairs={{0,8},{8,0},{16,24},{24,16},{1,9},{9,1},{17,25},{25,17},{2,10},{10... | collective-permute-start | bytes 1572872 | tf_op jit(solution)/shard_map/ppermute | solution.py:43
  2.5 15.5 %collective-permute-start.2 = (bf16[256,1024]{1,0:T(8,128)(2,1)}, bf16[256,1024]{1,0:T(8,128)(2,1)}, u32[]{:S(2)}, u32[]{:S(2)}) collective-permute-start(bf16[256,1024]{1,0:T(8,128)(2,1)} %shard_map.145.refs_2_.refs_3_), channel_id=1, source_target_pairs={{0,16},{8,24},{16,0},{24,8},{1,17},{9,25},{17,1},{25,9},{2,18},{10... | collective-permute-start | bytes 1572872 | tf_op jit(solution)/shard_map/ppermute | solution.py:43
  6.4 5.0 %collective-permute-start.1 = (s32[2,128]{1,0:T(2,128)S(1)}, s32[2,128]{1,0:T(2,128)S(1)}, u32[]{:S(2)}, u32[]{:S(2)}) collective-permute-start(s32[2,128]{1,0:T(2,128)S(1)} %get-tuple-element.39.refs_0_), channel_id=1, source_target_pairs={{0,4},{1,5},{2,6},{3,7},{4,0},{5,1},{6,2},{7,3},{8,12},{9,13},{10,... | collective-permute-start | bytes 3080 | tf_op jit(solution)/shard_map/ppermute | solution.py:43
  9.0 3.2 %collective-permute-start.6 = (s32[2,128]{1,0:T(2,128)S(1)}, s32[2,128]{1,0:T(2,128)S(1)}, u32[]{:S(2)}, u32[]{:S(2)}) collective-permute-start(s32[2,128]{1,0:T(2,128)S(1)} %get-tuple-element.40), channel_id=1, source_target_pairs={{0,8},{8,0},{16,24},{24,16},{1,9},{9,1},{17,25},{25,17},{2,10},{10... | collective-permute-start | bytes 3080 | tf_op jit(solution)/shard_map/ppermute | solution.py:43
  9.0 8.9 %collective-permute-start.7 = (s32[2,128]{1,0:T(2,128)S(1)}, s32[2,128]{1,0:T(2,128)S(1)}, u32[]{:S(2)}, u32[]{:S(2)}) collective-permute-start(s32[2,128]{1,0:T(2,128)S(1)} %get-tuple-element.40), channel_id=1, source_target_pairs={{0,16},{8,24},{16,0},{24,8},{1,17},{9,25},{17,1},{25,9},{2,18},{10... | collective-permute-start | bytes 3080 | tf_op jit(solution)/shard_map/ppermute | solution.py:43
  9.8 8.1 %collective-permute-start.3 = (s32[2,128]{1,0:T(2,128)S(1)}, s32[2,128]{1,0:T(2,128)S(1)}, u32[]{:S(2)}, u32[]{:S(2)}) collective-permute-start(s32[2,128]{1,0:T(2,128)S(1)} %get-tuple-element.39.refs_0_), channel_id=1, source_target_pairs={{0,2},{1,3},{2,0},{3,1},{4,6},{5,7},{6,4},{7,5},{8,10},{9,11},{10,... | collective-permute-start | bytes 3080 | tf_op jit(solution)/shard_map/ppermute | solution.py:43
  11.4 6.5 %collective-permute-start.5 = (s32[2,128]{1,0:T(2,128)S(1)}, s32[2,128]{1,0:T(2,128)S(1)}, u32[]{:S(2)}, u32[]{:S(2)}) collective-permute-start(s32[2,128]{1,0:T(2,128)S(1)} %get-tuple-element.40), channel_id=1, source_target_pairs={{0,24},{8,16},{16,8},{24,0},{1,25},{9,17},{17,9},{25,1},{2,26},{10... | collective-permute-start | bytes 3080 | tf_op jit(solution)/shard_map/ppermute | solution.py:43
  12.2 5.7 %collective-permute-start.4 = (s32[2,128]{1,0:T(2,128)S(1)}, s32[2,128]{1,0:T(2,128)S(1)}, u32[]{:S(2)}, u32[]{:S(2)}) collective-permute-start(s32[2,128]{1,0:T(2,128)S(1)} %collective-permute-done.1.refs_4_.refs_2_), channel_id=1, source_target_pairs={{0,2},{1,3},{2,0},{3,1},{4,6},{5,7},{6,4},{7,5},{8,10},{9,11},{10,... | collective-permute-start | bytes 3080 | tf_op jit(solution)/shard_map/ppermute | solution.py:43
  12.6 1.0 copy-start.6
  13.7 1.0 copy-start.7
  17.9 2.2 %collective-permute-start.8 = (bf16[256,1024]{1,0:T(8,128)(2,1)}, bf16[256,1024]{1,0:T(8,128)(2,1)S(1)}, u32[]{:S(2)}, u32[]{:S(2)}) collective-permute-start(bf16[256,1024]{1,0:T(8,128)(2,1)} %shard_map.149.refs_5_.refs_12_), channel_id=1, source_target_pairs={{0,8},{8,0},{16,24},{24,16},{1,9},{9,1},{17,25},{25,17},{2,10},{10... | collective-permute-start | bytes 1572872 | tf_op jit(solution)/shard_map/ppermute | solution.py:43
  24.1 15.2 %collective-permute-start.13 = (bf16[128,1024]{1,0:T(8,128)(2,1)S(1)}, bf16[128,1024]{1,0:T(8,128)(2,1)S(1)}, u32[]{:S(2)}, u32[]{:S(2)}) collective-permute-start(bf16[128,1024]{1,0:T(8,128)(2,1)S(1)} %get-tuple-element.47.refs_5_.refs_3_), channel_id=1, source_target_pairs={{0,4},{1,5},{2,6},{3,7},{4,0},{5,1},{6,2},{7,3},{8,12},{9,13},{10,... | collective-permute-start | bytes 786440 | tf_op jit(solution)/shard_map/ppermute | solution.py:43
  27.0 12.9 %collective-permute-start.12 = (bf16[128,1024]{1,0:T(8,128)(2,1)S(1)}, bf16[128,1024]{1,0:T(8,128)(2,1)S(1)}, u32[]{:S(2)}, u32[]{:S(2)}) collective-permute-start(bf16[128,1024]{1,0:T(8,128)(2,1)S(1)} %get-tuple-element.47.refs_5_.refs_3_), channel_id=1, source_target_pairs={{0,2},{1,3},{2,0},{3,1},{4,6},{5,7},{6,4},{7,5},{8,10},{9,11},{10,... | collective-permute-start | bytes 786440 | tf_op jit(solution)/shard_map/ppermute | solution.py:43
  28.6 20.1 %collective-permute-start.10 = (bf16[256,1024]{1,0:T(8,128)(2,1)S(1)}, bf16[256,1024]{1,0:T(8,128)(2,1)S(1)}, u32[]{:S(2)}, u32[]{:S(2)}) collective-permute-start(bf16[256,1024]{1,0:T(8,128)(2,1)S(1)} %shard_map.151.refs_7_.refs_4_), channel_id=1, source_target_pairs={{0,16},{8,24},{16,0},{24,8},{1,17},{9,25},{17,1},{25,9},{2,18},{10... | collective-permute-start | bytes 1572872 | tf_op jit(solution)/shard_map/ppermute | solution.py:43
  30.1 18.6 %collective-permute-start.11 = (bf16[256,1024]{1,0:T(8,128)(2,1)S(1)}, bf16[256,1024]{1,0:T(8,128)(2,1)S(1)}, u32[]{:S(2)}, u32[]{:S(2)}) collective-permute-start(bf16[256,1024]{1,0:T(8,128)(2,1)S(1)} %shard_map.151.refs_7_.refs_4_), channel_id=1, source_target_pairs={{0,0},{8,16},{16,8},{24,24},{1,1},{9,17},{17,9},{25,25},{2,2},{10,... | collective-permute-start | bytes 1572872 | tf_op jit(solution)/shard_map/ppermute | solution.py:580
  30.9 17.8 %collective-permute-start.9 = (bf16[256,1024]{1,0:T(8,128)(2,1)S(1)}, bf16[256,1024]{1,0:T(8,128)(2,1)S(1)}, u32[]{:S(2)}, u32[]{:S(2)}) collective-permute-start(bf16[256,1024]{1,0:T(8,128)(2,1)S(1)} %shard_map.151.refs_7_.refs_4_), channel_id=1, source_target_pairs={{0,8},{8,0},{16,24},{24,16},{1,9},{9,1},{17,25},{25,17},{2,10},{10... | collective-permute-start | bytes 1572872 | tf_op jit(solution)/shard_map/ppermute | solution.py:43
  39.3 7.7 %collective-permute-start.14 = (bf16[128,1024]{1,0:T(8,128)(2,1)S(1)}, bf16[128,1024]{1,0:T(8,128)(2,1)S(1)}, u32[]{:S(2)}, u32[]{:S(2)}) collective-permute-start(bf16[128,1024]{1,0:T(8,128)(2,1)S(1)} %collective-permute-done.13.refs_1_.refs_5_), channel_id=1, source_target_pairs={{0,2},{1,3},{2,0},{3,1},{4,6},{5,7},{6,4},{7,5},{8,10},{9,11},{10,... | collective-permute-start | bytes 786440 | tf_op jit(solution)/shard_map/ppermute | solution.py:43
  39.9 8.8 %copy-start.9 = (bf16[1024,8]{0,1:T(8,128)(2,1)S(1)}, bf16[1024,8]{0,1:T(8,128)(2,1)}, u32[]{:S(2)}) copy-start(bf16[1024,8]{0,1:T(8,128)(2,1)} %param.22) | copy-start | bytes 49156
  39.9 17.3 %copy-start.2 = (bf16[1,1408,1024]{2,1,0:T(8,128)(2,1)S(1)}, bf16[1,1408,1024]{2,1,0:T(8,128)(2,1)}, u32[]{:S(2)}) copy-start(bf16[1,1408,1024]{2,1,0:T(8,128)(2,1)} %refs_7_.1) | copy-start | bytes 8650756
  40.4 16.9 %collective-permute-start.18 = (bf16[160,1024]{1,0:T(8,128)(2,1)S(1)}, bf16[160,1024]{1,0:T(8,128)(2,1)S(1)}, u32[]{:S(2)}, u32[]{:S(2)}) collective-permute-start(bf16[160,1024]{1,0:T(8,128)(2,1)S(1)} %get-tuple-element.56), channel_id=1, source_target_pairs={{0,1},{1,0},{2,3},{3,2},{4,5},{5,4},{6,7},{7,6},{8,9},{9,8},{10,11... | collective-permute-start | bytes 983048 | tf_op jit(solution)/shard_map/ppermute | solution.py:43
  47.0 10.3 %copy-start.1 = (bf16[1,1024,1408]{2,1,0:T(8,128)(2,1)S(1)}, bf16[1,1024,1408]{2,1,0:T(8,128)(2,1)}, u32[]{:S(2)}) copy-start(bf16[1,1024,1408]{2,1,0:T(8,128)(2,1)} %refs_6_.1) | copy-start | bytes 8650756
  47.3 10.0 %copy-start = (bf16[1,1024,1408]{2,1,0:T(8,128)(2,1)S(1)}, bf16[1,1024,1408]{2,1,0:T(8,128)(2,1)}, u32[]{:S(2)}) copy-start(bf16[1,1024,1408]{2,1,0:T(8,128)(2,1)} %refs_5_.1) | copy-start | bytes 8650756
  47.3 10.0 %collective-permute-start.19 = (bf16[160,1024]{1,0:T(8,128)(2,1)S(1)}, bf16[160,1024]{1,0:T(8,128)(2,1)S(1)}, u32[]{:S(2)}, u32[]{:S(2)}) collective-permute-start(bf16[160,1024]{1,0:T(8,128)(2,1)S(1)} %shard_map.153.refs_13_), channel_id=1, source_target_pairs={{0,1},{1,0},{2,3},{3,2},{4,5},{5,4},{6,7},{7,6},{8,9},{9,8},{10,11... | collective-permute-start | bytes 983048 | tf_op jit(solution)/shard_map/ppermute | solution.py:43
  52.4 13.3 %collective-permute-start.15 = (bf16[80,1024]{1,0:T(8,128)(2,1)S(1)}, bf16[80,1024]{1,0:T(8,128)(2,1)S(1)}, u32[]{:S(2)}, u32[]{:S(2)}) collective-permute-start(bf16[80,1024]{1,0:T(8,128)(2,1)S(1)} %get-tuple-element.52), channel_id=1, source_target_pairs={{0,6},{1,7},{2,4},{3,5},{4,2},{5,3},{6,0},{7,1},{8,14},{9,15},{10,... | collective-permute-start | bytes 491528 | tf_op jit(solution)/shard_map/ppermute | solution.py:43
  56.6 12.9 %collective-permute-start.16 = (bf16[80,1024]{1,0:T(8,128)(2,1)S(1)}, bf16[80,1024]{1,0:T(8,128)(2,1)S(1)}, u32[]{:S(2)}, u32[]{:S(2)}) collective-permute-start(bf16[80,1024]{1,0:T(8,128)(2,1)S(1)} %get-tuple-element.53), channel_id=1, source_target_pairs={{0,4},{1,5},{2,6},{3,7},{4,0},{5,1},{6,2},{7,3},{8,12},{9,13},{10,... | collective-permute-start | bytes 491528 | tf_op jit(solution)/shard_map/ppermute | solution.py:43
  56.6 12.9 %collective-permute-start.17 = (bf16[80,1024]{1,0:T(8,128)(2,1)S(1)}, bf16[80,1024]{1,0:T(8,128)(2,1)S(1)}, u32[]{:S(2)}, u32[]{:S(2)}) collective-permute-start(bf16[80,1024]{1,0:T(8,128)(2,1)S(1)} %get-tuple-element.54), channel_id=1, source_target_pairs={{0,2},{1,3},{2,0},{3,1},{4,6},{5,7},{6,4},{7,5},{8,10},{9,11},{10,... | collective-permute-start | bytes 491528 | tf_op jit(solution)/shard_map/ppermute | solution.py:43
  60.6 9.5 %collective-permute-start.21 = (bf16[160,1024]{1,0:T(8,128)(2,1)S(1)}, bf16[160,1024]{1,0:T(8,128)(2,1)S(1)}, u32[]{:S(2)}, u32[]{:S(2)}) collective-permute-start(bf16[160,1024]{1,0:T(8,128)(2,1)S(1)} %get-tuple-element.60), channel_id=1, source_target_pairs={{0,1},{1,0},{2,3},{3,2},{4,5},{5,4},{6,7},{7,6},{8,9},{9,8},{10,11... | collective-permute-start | bytes 983048 | tf_op jit(solution)/shard_map/ppermute | solution.py:43
  69.6 8.8 %collective-permute-start.20 = (bf16[160,1024]{1,0:T(8,128)(2,1)S(1)}, bf16[160,1024]{1,0:T(8,128)(2,1)S(1)}, u32[]{:S(2)}, u32[]{:S(2)}) collective-permute-start(bf16[160,1024]{1,0:T(8,128)(2,1)S(1)} %shard_map.157.refs_4_), channel_id=1, source_target_pairs={{0,1},{1,0},{2,3},{3,2},{4,5},{5,4},{6,7},{7,6},{8,9},{9,8},{10,11... | collective-permute-start | bytes 983048 | tf_op jit(solution)/shard_map/ppermute | solution.py:43
  70.9 12.9 %collective-permute-start.24 = (bf16[128,1024]{1,0:T(8,128)(2,1)S(1)}, bf16[128,1024]{1,0:T(8,128)(2,1)S(1)}, u32[]{:S(2)}, u32[]{:S(2)}) collective-permute-start(bf16[128,1024]{1,0:T(8,128)(2,1)S(1)} %get-tuple-element.64), channel_id=1, source_target_pairs={{0,2},{1,3},{2,0},{3,1},{4,6},{5,7},{6,4},{7,5},{8,10},{9,11},{10,... | collective-permute-start | bytes 786440 | tf_op jit(solution)/shard_map/ppermute | solution.py:43
  78.4 10.6 %collective-permute-start.23 = (bf16[160,1024]{1,0:T(8,128)(2,1)S(1)}, bf16[160,1024]{1,0:T(8,128)(2,1)S(1)}, u32[]{:S(2)}, u32[]{:S(2)}) collective-permute-start(bf16[160,1024]{1,0:T(8,128)(2,1)S(1)} %shard_map.159.refs_8_), channel_id=1, source_target_pairs={{0,1},{1,0},{2,3},{3,2},{4,5},{5,4},{6,7},{7,6},{8,9},{9,8},{10,11... | collective-permute-start | bytes 983048 | tf_op jit(solution)/shard_map/ppermute | solution.py:43
  82.0 11.2 %collective-permute-start.22 = (bf16[160,1024]{1,0:T(8,128)(2,1)S(1)}, bf16[160,1024]{1,0:T(8,128)(2,1)S(1)}, u32[]{:S(2)}, u32[]{:S(2)}) collective-permute-start(bf16[160,1024]{1,0:T(8,128)(2,1)S(1)} %get-tuple-element.63), channel_id=1, source_target_pairs={{0,1},{1,0},{2,3},{3,2},{4,5},{5,4},{6,7},{7,6},{8,9},{9,8},{10,11... | collective-permute-start | bytes 983048 | tf_op jit(solution)/shard_map/ppermute | solution.py:43
  83.9 13.8 %collective-permute-start.28 = (bf16[128,1024]{1,0:T(8,128)(2,1)S(1)}, bf16[128,1024]{1,0:T(8,128)(2,1)S(1)}, u32[]{:S(2)}, u32[]{:S(2)}) collective-permute-start(bf16[128,1024]{1,0:T(8,128)(2,1)S(1)} %shard_map.161.refs_4_), channel_id=1, source_target_pairs={{0,4},{1,5},{2,6},{3,7},{4,0},{5,1},{6,2},{7,3},{8,12},{9,13},{10,... | collective-permute-start | bytes 786440 | tf_op jit(solution)/shard_map/ppermute | solution.py:43
  89.8 18.4 %collective-permute-start.29 = (bf16[128,1024]{1,0:T(8,128)(2,1)S(1)}, bf16[128,1024]{1,0:T(8,128)(2,1)S(1)}, u32[]{:S(2)}, u32[]{:S(2)}) collective-permute-start(bf16[128,1024]{1,0:T(8,128)(2,1)S(1)} %get-tuple-element.70), channel_id=1, source_target_pairs={{0,2},{1,3},{2,0},{3,1},{4,6},{5,7},{6,4},{7,5},{8,10},{9,11},{10,... | collective-permute-start | bytes 786440 | tf_op jit(solution)/shard_map/ppermute | solution.py:43
  93.2 9.0 %collective-permute-start.25 = (bf16[80,1024]{1,0:T(8,128)(2,1)S(1)}, bf16[80,1024]{1,0:T(8,128)(2,1)S(1)}, u32[]{:S(2)}, u32[]{:S(2)}) collective-permute-start(bf16[80,1024]{1,0:T(8,128)(2,1)S(1)} %get-tuple-element.66), channel_id=1, source_target_pairs={{0,6},{1,7},{2,4},{3,5},{4,2},{5,3},{6,0},{7,1},{8,14},{9,15},{10,... | collective-permute-start | bytes 491528 | tf_op jit(solution)/shard_map/ppermute | solution.py:43
  94.1 14.1 %collective-permute-start.26 = (bf16[80,1024]{1,0:T(8,128)(2,1)S(1)}, bf16[80,1024]{1,0:T(8,128)(2,1)S(1)}, u32[]{:S(2)}, u32[]{:S(2)}) collective-permute-start(bf16[80,1024]{1,0:T(8,128)(2,1)S(1)} %get-tuple-element.67), channel_id=1, source_target_pairs={{0,4},{1,5},{2,6},{3,7},{4,0},{5,1},{6,2},{7,3},{8,12},{9,13},{10,... | collective-permute-start | bytes 491528 | tf_op jit(solution)/shard_map/ppermute | solution.py:43
  94.9 13.2 %collective-permute-start.27 = (bf16[80,1024]{1,0:T(8,128)(2,1)S(1)}, bf16[80,1024]{1,0:T(8,128)(2,1)S(1)}, u32[]{:S(2)}, u32[]{:S(2)}) collective-permute-start(bf16[80,1024]{1,0:T(8,128)(2,1)S(1)} %get-tuple-element.68), channel_id=1, source_target_pairs={{0,2},{1,3},{2,0},{3,1},{4,6},{5,7},{6,4},{7,5},{8,10},{9,11},{10,... | collective-permute-start | bytes 491528 | tf_op jit(solution)/shard_map/ppermute | solution.py:43
where the time goes:
time: 110 us
  waiting for transfers between devices  45.6 us (41%)
  starting transfers between devices  36.2 us (33%)
  Pallas kernels  22.8 us (21%)
  local copies, waits for them, and re-layouts  4.67 us (4%)
    ppermute x29, waiting for transfers between devices, swapped(): lax.ppermute(value, axis, [(source, source ^ mask) for source in range(co...  45.6 us
    ppermute x29, starting transfers between devices, swapped(): lax.ppermute(value, axis, [(source, source ^ mask) for source in range(co...  35.3 us
    pallas_call x21, Pallas kernels, call(): pl.pallas_call(body, out_shape=outs, in_specs=ins + [ANY] * len(after), o...  22.8 us
  transfers between devices with their start and end apart: 30, of which 10 were waited for; matrix products, arithmetic and copies ran while one was open for 1% of the time, Pallas kernels for 15%

commit v1 on v0

--- a/solution.py
+++ b/solution.py
@@ -340,20 +340,24 @@
     expert_rows(rows, weights, active, stores)
 
 
-def direct_kernel(layers, *refs):
-    packets, crossed, weights = (refs[:layers][::-1], refs[layers], refs[layers + 1 : layers + 4])
-    near, far, rows, active = refs[layers + 4 :]
+def direct_near_kernel(layers, *refs):
+    packets, weights = (refs[:layers][::-1], refs[layers : layers + 3])
+    out, rows, active = refs[layers + 3 :]
     cap = packets[0].shape[0] // 2
-    half = layers * cap
 
     def stores(span, value):
-        near[:, span] = value[:half].astype(bf16)
-        far[:, span] = value[half:].astype(bf16)
+        out[:, span] = value.astype(bf16)
 
     parts = [ref[...].astype(f32)[:cap] for ref in packets]
-    rows[:half, :] = jnp.concatenate(parts, axis=0).astype(bf16)
-    rows[half:, :] = crossed[...]
+    rows[...] = jnp.concatenate(parts, axis=0).astype(bf16)
     expert_rows(rows, weights, active, stores)
+
+
+def direct_far_kernel(crossed, gate, up, down, out, active):
+    def stores(span, value):
+        out[:, span] = value.astype(bf16)
+
+    expert_rows(crossed, (gate, up, down), active, stores)
 
 
 def rejoin_kernel(near, far, *outs):
@@ -429,6 +433,7 @@
     cap_two = capacity * MAX_SLOTS
     slots = columns * cap_two
     part_two = slots // 2
+    half_one = columns * capacity
     packet = shaped((2 * capacity, width), bf16)
     stack_shape = shaped((2 * tok_count, width), bf16)
     latest = []
@@ -615,17 +620,18 @@
     totals = {}
     partial(upper, high_far)
     send_down(m for m in upper if m % 2)
+    near_one = call(
+        functools.partial(direct_near_kernel, columns), shaped((half_one, width), bf16),
+        [VMEM] * (3 + columns), (*arrived[::-1], *weights), scratch=scratch_for(half_one),
+    )
     (low_out,) = call(
         pass_kernel, (shaped(low_out.shape, bf16),), [ANY], (low_out,), aliases={0: 0},
         after=[crossed_one],
     )
     low_far = swapped(low_out, "exp", 1)
-    near_one, far_one = call(
-        functools.partial(direct_kernel, columns),
-        (shaped((columns * capacity, width), bf16),) * 2,
-        [VMEM] * (4 + columns),
-        (*arrived[::-1], crossed_one, *weights),
-        scratch=scratch_for(experts * capacity),
+    far_one = call(
+        direct_far_kernel, shaped((half_one, width), bf16), [VMEM] * 4, (crossed_one, *weights),
+        scratch=scratch_for(half_one)[1:],
     )
     far_one = swapped(far_one, "exp", 1)
     send_down(m for m in upper if m % 2 == 0)

time: 110 us -> 109 us (level)
    pallas_call x21 -> x22, Pallas kernels: 22.8 us -> 23 us  [call(): pl.pallas_call(body, out_shape=outs, in_specs=ins + [ANY] * len(after), o...]
  transfers between devices with their start and end apart: 30 -> 30, of which waited for: 10 -> 10; matrix products, arithmetic and copies ran while one was open for 1% -> 1% of each run, Pallas kernels for 15% -> 16%
where the time goes in v1:
time: 109 us
  waiting for transfers between devices  44.7 us (41%)
  starting transfers between devices  36.2 us (33%)
  Pallas kernels  23 us (21%)
  local copies, waits for them, and re-layouts  4.67 us (4%)
    ppermute x29, waiting for transfers between devices, swapped(): lax.ppermute(value, axis, [(source, source ^ mask) for source in range(co...  44.7 us
    ppermute x29, starting transfers between devices, swapped(): lax.ppermute(value, axis, [(source, source ^ mask) for source in range(co...  35.3 us
    pallas_call x22, Pallas kernels, call(): pl.pallas_call(body, out_shape=outs, in_specs=ins + [ANY] * len(after), o...  23 us
  transfers between devices with their start and end apart: 30, of which 10 were waited for; matrix products, arithmetic and copies ran while one was open for 1% of the time, Pallas kernels for 16%

profile of v1, /device:TPU:0, one launch (start us, length us, event | category | flops | bytes accessed | tf_op | source)
XLA Modules:
  0.0 108.8 jit_solution(5456866267849605266)
XLA Ops:
  0.0 1.2 %slice_bitcast_fusion = (bf16[128,1024]{1,0:T(8,128)(2,1)S(1)}, bf16[128,1024]{1,0:T(8,128)(2,1)S(1)}) fusion(bf16[2,1,128,1024]{3,2,1,0:T(8,128)(2,1)} %refs_1_.2, bf16[2,1,128,1024]{3,2,1,0:T(8,128)(2,1)} %refs_0_.3), kind=kLoop, calls=%fused_computation | loop fusion | bytes 1048576 | tf_op jit(solution)/shard_map/squeeze | solution.py:540
  1.2 0.0 copy-start.8
  1.2 0.8 shard_map.145.refs_2_.refs_3_
  2.0 0.5 collective-permute-start
  2.5 2.5 %collective-permute-start.2 = (bf16[256,1024]{1,0:T(8,128)(2,1)}, bf16[256,1024]{1,0:T(8,128)(2,1)}, u32[]{:S(2)}, u32[]{:S(2)}) collective-permute-start(bf16[256,1024]{1,0:T(8,128)(2,1)} %shard_map.145.refs_2_.refs_3_), channel_id=1, source_target_pairs={{0,16},{8,24},{16,0},{24,8},{1,17},{9,25},{17,1},{25,9},{2,18},{10... | collective-permute-start | bytes 1572872 | tf_op jit(solution)/shard_map/ppermute | solution.py:43
  4.9 0.7 pad_bitcast_fusion
  5.6 0.7 concatenate.3.refs_0_
  6.4 2.7 %collective-permute-start.1 = (s32[2,128]{1,0:T(2,128)S(1)}, s32[2,128]{1,0:T(2,128)S(1)}, u32[]{:S(2)}, u32[]{:S(2)}) collective-permute-start(s32[2,128]{1,0:T(2,128)S(1)} %get-tuple-element.37.refs_0_), channel_id=1, source_target_pairs={{0,4},{1,5},{2,6},{3,7},{4,0},{5,1},{6,2},{7,3},{8,12},{9,13},{10,... | collective-permute-start | bytes 3080 | tf_op jit(solution)/shard_map/ppermute | solution.py:43
  9.0 0.0 collective-permute-start.6
  9.0 0.8 collective-permute-start.7
  9.8 1.6 %collective-permute-start.3 = (s32[2,128]{1,0:T(2,128)S(1)}, s32[2,128]{1,0:T(2,128)S(1)}, u32[]{:S(2)}, u32[]{:S(2)}) collective-permute-start(s32[2,128]{1,0:T(2,128)S(1)} %get-tuple-element.37.refs_0_), channel_id=1, source_target_pairs={{0,2},{1,3},{2,0},{3,1},{4,6},{5,7},{6,4},{7,5},{8,10},{9,11},{10,... | collective-permute-start | bytes 3080 | tf_op jit(solution)/shard_map/ppermute | solution.py:43
  11.4 0.8 collective-permute-start.5
  12.2 0.0 collective-permute-done.6.refs_5_.refs_7_.refs_8_
  12.2 0.5 collective-permute-start.4
  12.6 1.0 copy-done.6
  13.7 1.0 copy-done.7
  14.8 3.1 %collective-permute-done.7.refs_6_.refs_8_.refs_9_ = s32[2,128]{1,0:T(2,128)S(1)} collective-permute-done((s32[2,128]{1,0:T(2,128)S(1)}, s32[2,128]{1,0:T(2,128)S(1)}, u32[]{:S(2)}, u32[]{:S(2)}) %collective-permute-start.7) | collective-permute-done | bytes 1056 | tf_op jit(solution)/shard_map/ppermute | solution.py:43
  17.9 0.0 collective-permute-done.4.refs_3_
  17.9 0.2 collective-permute-start.8
  18.1 2.0 %collective-permute-done.8.refs_6_ = bf16[256,1024]{1,0:T(8,128)(2,1)S(1)} collective-permute-done((bf16[256,1024]{1,0:T(8,128)(2,1)}, bf16[256,1024]{1,0:T(8,128)(2,1)S(1)}, u32[]{:S(2)}, u32[]{:S(2)}) %collective-permute-start.8) | collective-permute-done | bytes 524320 | tf_op jit(solution)/shard_map/ppermute | solution.py:43
  20.1 4.0 %shard_map.150 = (f32[128,1024]{1,0:T(8,128)S(1)}, bf16[128,1024]{1,0:T(8,128)(2,1)S(1)}) custom-call(f32[16,32]{1,0:T(8,128)S(1)} %copy-done.8, s32[8,128]{1,0:T(8,128)S(1)} %get-tuple-element.36.refs_5_.refs_1_.refs_0_.refs_2_, bf16[2,1,128,1024]{3,2,1,0:T(8,128)(2,1)S(1)} %copy-done.4, bf16[256,1024]{1,0:T(8,128)(2,1)} %shard_map.145.refs_2_.refs_3_, ...), custom_call_target="tpu_custom_call" | custom-call | flops 1 | bytes 1 | tf_op jit(solution)/shard_map/pallas_call | solution.py:450
  24.1 2.9 %collective-permute-start.13 = (bf16[128,1024]{1,0:T(8,128)(2,1)S(1)}, bf16[128,1024]{1,0:T(8,128)(2,1)S(1)}, u32[]{:S(2)}, u32[]{:S(2)}) collective-permute-start(bf16[128,1024]{1,0:T(8,128)(2,1)S(1)} %get-tuple-element.45.refs_5_.refs_3_), channel_id=1, source_target_pairs={{0,4},{1,5},{2,6},{3,7},{4,0},{5,1},{6,2},{7,3},{8,12},{9,13},{10,... | collective-permute-start | bytes 786440 | tf_op jit(solution)/shard_map/ppermute | solution.py:43
  27.0 1.6 %collective-permute-start.12 = (bf16[128,1024]{1,0:T(8,128)(2,1)S(1)}, bf16[128,1024]{1,0:T(8,128)(2,1)S(1)}, u32[]{:S(2)}, u32[]{:S(2)}) collective-permute-start(bf16[128,1024]{1,0:T(8,128)(2,1)S(1)} %get-tuple-element.45.refs_5_.refs_3_), channel_id=1, source_target_pairs={{0,2},{1,3},{2,0},{3,1},{4,6},{5,7},{6,4},{7,5},{8,10},{9,11},{10,... | collective-permute-start | bytes 786440 | tf_op jit(solution)/shard_map/ppermute | solution.py:43
  28.6 1.5 %collective-permute-start.10 = (bf16[256,1024]{1,0:T(8,128)(2,1)S(1)}, bf16[256,1024]{1,0:T(8,128)(2,1)S(1)}, u32[]{:S(2)}, u32[]{:S(2)}) collective-permute-start(bf16[256,1024]{1,0:T(8,128)(2,1)S(1)} %shard_map.151.refs_7_.refs_4_), channel_id=1, source_target_pairs={{0,16},{8,24},{16,0},{24,8},{1,17},{9,25},{17,1},{25,9},{2,18},{10... | collective-permute-start | bytes 1572872 | tf_op jit(solution)/shard_map/ppermute | solution.py:43
  30.1 0.9 collective-permute-start.11
  30.9 1.9 %collective-permute-start.9 = (bf16[256,1024]{1,0:T(8,128)(2,1)S(1)}, bf16[256,1024]{1,0:T(8,128)(2,1)S(1)}, u32[]{:S(2)}, u32[]{:S(2)}) collective-permute-start(bf16[256,1024]{1,0:T(8,128)(2,1)S(1)} %shard_map.151.refs_7_.refs_4_), channel_id=1, source_target_pairs={{0,8},{8,0},{16,24},{24,16},{1,9},{9,1},{17,25},{25,17},{2,10},{10... | collective-permute-start | bytes 1572872 | tf_op jit(solution)/shard_map/ppermute | solution.py:43
  32.9 6.5 %collective-permute-done.13.refs_1_.refs_5_ = bf16[128,1024]{1,0:T(8,128)(2,1)S(1)} collective-permute-done((bf16[128,1024]{1,0:T(8,128)(2,1)S(1)}, bf16[128,1024]{1,0:T(8,128)(2,1)S(1)}, u32[]{:S(2)}, u32[]{:S(2)}) %collective-permute-start.13) | collective-permute-done | bytes 262176 | tf_op jit(solution)/shard_map/ppermute | solution.py:43
  39.3 0.6 collective-permute-start.14
  39.9 0.5 shard_map.152
  40.4 1.6 %collective-permute-start.18 = (bf16[160,1024]{1,0:T(8,128)(2,1)S(1)}, bf16[160,1024]{1,0:T(8,128)(2,1)S(1)}, u32[]{:S(2)}, u32[]{:S(2)}) collective-permute-start(bf16[160,1024]{1,0:T(8,128)(2,1)S(1)} %get-tuple-element.54), channel_id=1, source_target_pairs={{0,1},{1,0},{2,3},{3,2},{4,5},{5,4},{6,7},{7,6},{8,9},{9,8},{10,11... | collective-permute-start | bytes 983048 | tf_op jit(solution)/shard_map/ppermute | solution.py:43
  42.0 5.0 %collective-permute-done.14.refs_2_.refs_6_ = bf16[128,1024]{1,0:T(8,128)(2,1)S(1)} collective-permute-done((bf16[128,1024]{1,0:T(8,128)(2,1)S(1)}, bf16[128,1024]{1,0:T(8,128)(2,1)S(1)}, u32[]{:S(2)}, u32[]{:S(2)}) %collective-permute-start.14) | collective-permute-done | bytes 262176 | tf_op jit(solution)/shard_map/ppermute | solution.py:43
  47.0 0.2 shard_map.153.refs_13_
  47.3 0.0 copy-start
  47.3 1.4 %collective-permute-start.19 = (bf16[160,1024]{1,0:T(8,128)(2,1)S(1)}, bf16[160,1024]{1,0:T(8,128)(2,1)S(1)}, u32[]{:S(2)}, u32[]{:S(2)}) collective-permute-start(bf16[160,1024]{1,0:T(8,128)(2,1)S(1)} %shard_map.153.refs_13_), channel_id=1, source_target_pairs={{0,1},{1,0},{2,3},{3,2},{4,5},{5,4},{6,7},{7,6},{8,9},{9,8},{10,11... | collective-permute-start | bytes 983048 | tf_op jit(solution)/shard_map/ppermute | solution.py:43
  48.7 0.0 collective-permute-done.11.refs_7_
  48.7 0.0 collective-permute-done.9.refs_5_
  48.7 3.7 %shard_map.154 = (bf16[80,1024]{1,0:T(8,128)(2,1)S(1)}, bf16[80,1024]{1,0:T(8,128)(2,1)S(1)}, bf16[80,1024]{1,0:T(8,128)(2,1)S(1)}, bf16[80,1024]{1,0:T(8,128)(2...) custom-call(f32[16,32]{1,0:T(8,128)S(1)} %copy-done.8, ...), custom_call_target="tpu_custom_call" | custom-call | flops 1 | bytes 1 | tf_op jit(solution)/shard_map/pallas_call | solution.py:450
  52.4 4.2 %collective-permute-start.15 = (bf16[80,1024]{1,0:T(8,128)(2,1)S(1)}, bf16[80,1024]{1,0:T(8,128)(2,1)S(1)}, u32[]{:S(2)}, u32[]{:S(2)}) collective-permute-start(bf16[80,1024]{1,0:T(8,128)(2,1)S(1)} %get-tuple-element.50), channel_id=1, source_target_pairs={{0,6},{1,7},{2,4},{3,5},{4,2},{5,3},{6,0},{7,1},{8,14},{9,15},{10,... | collective-permute-start | bytes 491528 | tf_op jit(solution)/shard_map/ppermute | solution.py:43
  56.6 0.0 collective-permute-start.16
  56.6 0.6 collective-permute-start.17
  57.3 3.3 %shard_map.155 = (bf16[160,1024]{1,0:T(8,128)(2,1)S(1)}, bf16[160,1024]{1,0:T(8,128)(2,1)S(1)}) custom-call(bf16[160,1024]{1,0:T(8,128)(2,1)S(1)} %collective-permute-done.18.refs_0_, bf16[160,1024]{1,0:T(8,128)(2,1)S(1)} %collective-permute-done.19.refs_1_, bf16[1,1024,1408]{2,1,0:T(8,128)(2,1)S(1)} %copy-done, bf16[1,1024,1408]{2,1,0:T(8,128)(2,1)S(1)} %copy-done.1, ...), custom_call_target="tpu_custom_call" | custom-call | flops 1 | bytes 1 | tf_op jit(solution)/shard_map/pallas_call | solution.py:450
  60.6 1.2 %collective-permute-start.20 = (bf16[160,1024]{1,0:T(8,128)(2,1)S(1)}, bf16[160,1024]{1,0:T(8,128)(2,1)S(1)}, u32[]{:S(2)}, u32[]{:S(2)}) collective-permute-start(bf16[160,1024]{1,0:T(8,128)(2,1)S(1)} %get-tuple-element.58), channel_id=1, source_target_pairs={{0,1},{1,0},{2,3},{3,2},{4,5},{5,4},{6,7},{7,6},{8,9},{9,8},{10,11... | collective-permute-start | bytes 983048 | tf_op jit(solution)/shard_map/ppermute | solution.py:43
  61.8 3.9 %shard_map.156 = (bf16[320,1024]{1,0:T(8,128)(2,1)S(1)}, f32[8,128]{1,0:T(8,128)S(1)}) custom-call(s32[8,128]{1,0:T(8,128)S(1)} %get-tuple-element.36.refs_5_.refs_1_.refs_0_.refs_2_, s32[8,128]{1,0:T(8,128)S(1)} %get-tuple-element.46.refs_0_.refs_3_.refs_1_, bf16[8,1024]{1,0:T(8,128)(2,1)S(1)} %bitcast.17, ...), custom_call_target="tpu_custom_call" | custom-call | flops 4000000000 | bytes 1 | tf_op jit(solution)/shard_map/pallas_call | solution.py:450
  65.7 3.9 %collective-permute-done.16.refs_1_ = bf16[80,1024]{1,0:T(8,128)(2,1)S(1)} collective-permute-done((bf16[80,1024]{1,0:T(8,128)(2,1)S(1)}, bf16[80,1024]{1,0:T(8,128)(2,1)S(1)}, u32[]{:S(2)}, u32[]{:S(2)}) %collective-permute-start.16) | collective-permute-done | bytes 163872 | tf_op jit(solution)/shard_map/ppermute | solution.py:43
  69.6 0.6 collective-permute-start.21
  70.2 0.7 shard_map.158
  70.9 0.1 collective-permute-start.24
  71.0 1.8 %shard_map.159.refs_2_.refs_0_ = bf16[160,1024]{1,0:T(8,128)(2,1)S(1)} custom-call(bf16[80,1024]{1,0:T(8,128)(2,1)S(1)} %collective-permute-done.15.refs_0_, bf16[80,1024]{1,0:T(8,128)(2,1)S(1)} %collective-permute-done.16.refs_1_, bf16[80,1024]{1,0:T(8,128)(2,1)S(1)} %collective-permute-done.17.refs_2_, ...), custom_call_target="tpu_custom_call" | custom-call | flops 1 | bytes 1 | tf_op jit(solution)/shard_map/pallas_call | solution.py:450
  72.8 5.6 %collective-permute-done.21.refs_1_.refs_0_ = bf16[160,1024]{1,0:T(8,128)(2,1)S(1)} collective-permute-done((bf16[160,1024]{1,0:T(8,128)(2,1)S(1)}, bf16[160,1024]{1,0:T(8,128)(2,1)S(1)}, u32[]{:S(2)}, u32[]{:S(2)}) %collective-permute-start.21) | collective-permute-done | bytes 327712 | tf_op jit(solution)/shard_map/ppermute | solution.py:43
  78.4 0.3 collective-permute-start.23
  78.7 1.8 %shard_map.161.refs_2_ = bf16[160,1024]{1,0:T(8,128)(2,1)S(1)} custom-call(bf16[160,1024]{1,0:T(8,128)(2,1)S(1)} %collective-permute-done.21.refs_1_.refs_0_, bf16[1,1024,1408]{2,1,0:T(8,128)(2,1)S(1)} %copy-done, bf16[1,1024,1408]{2,1,0:T(8,128)(2,1)S(1)} %copy-done.1, bf16[1,1408,1024]{2,1,0:T(8,128)(2,1)S(1)} %copy-done.2, ...), custom_call_target="tpu_custom_call" | custom-call | flops 1 | bytes 1 | tf_op jit(solution)/shard_map/pallas_call | solution.py:450
  80.5 1.8 %collective-permute-start.22 = (bf16[160,1024]{1,0:T(8,128)(2,1)S(1)}, bf16[160,1024]{1,0:T(8,128)(2,1)S(1)}, u32[]{:S(2)}, u32[]{:S(2)}) collective-permute-start(bf16[160,1024]{1,0:T(8,128)(2,1)S(1)} %shard_map.161.refs_2_), channel_id=1, source_target_pairs={{0,1},{1,0},{2,3},{3,2},{4,5},{5,4},{6,7},{7,6},{8,9},{9,8},{10,11... | collective-permute-start | bytes 983048 | tf_op jit(solution)/shard_map/ppermute | solution.py:43
  82.3 0.1 shard_map.162.refs_4_
  82.3 1.2 %collective-permute-start.28 = (bf16[128,1024]{1,0:T(8,128)(2,1)S(1)}, bf16[128,1024]{1,0:T(8,128)(2,1)S(1)}, u32[]{:S(2)}, u32[]{:S(2)}) collective-permute-start(bf16[128,1024]{1,0:T(8,128)(2,1)S(1)} %shard_map.162.refs_4_), channel_id=1, source_target_pairs={{0,4},{1,5},{2,6},{3,7},{4,0},{5,1},{6,2},{7,3},{8,12},{9,13},{10,... | collective-permute-start | bytes 786440 | tf_op jit(solution)/shard_map/ppermute | solution.py:43
  83.5 5.5 %collective-permute-done.23.refs_3_ = bf16[160,1024]{1,0:T(8,128)(2,1)S(1)} collective-permute-done((bf16[160,1024]{1,0:T(8,128)(2,1)S(1)}, bf16[160,1024]{1,0:T(8,128)(2,1)S(1)}, u32[]{:S(2)}, u32[]{:S(2)}) %collective-permute-start.23) | collective-permute-done | bytes 327712 | tf_op jit(solution)/shard_map/ppermute | solution.py:43
  89.0 0.7 shard_map.163
  89.8 0.1 collective-permute-start.29
  89.9 3.3 %collective-permute-done.22.refs_1_ = bf16[160,1024]{1,0:T(8,128)(2,1)S(1)} collective-permute-done((bf16[160,1024]{1,0:T(8,128)(2,1)S(1)}, bf16[160,1024]{1,0:T(8,128)(2,1)S(1)}, u32[]{:S(2)}, u32[]{:S(2)}) %collective-permute-start.22) | collective-permute-done | bytes 327712 | tf_op jit(solution)/shard_map/ppermute | solution.py:43
  93.2 0.9 collective-permute-start.25
  94.1 0.8 collective-permute-start.26
  94.9 2.8 %collective-permute-start.27 = (bf16[80,1024]{1,0:T(8,128)(2,1)S(1)}, bf16[80,1024]{1,0:T(8,128)(2,1)S(1)}, u32[]{:S(2)}, u32[]{:S(2)}) collective-permute-start(bf16[80,1024]{1,0:T(8,128)(2,1)S(1)} %get-tuple-element.64), channel_id=1, source_target_pairs={{0,2},{1,3},{2,0},{3,1},{4,6},{5,7},{6,4},{7,5},{8,10},{9,11},{10,... | collective-permute-start | bytes 491528 | tf_op jit(solution)/shard_map/ppermute | solution.py:43
  97.7 4.5 %collective-permute-done.25.refs_3_ = bf16[80,1024]{1,0:T(8,128)(2,1)S(1)} collective-permute-done((bf16[80,1024]{1,0:T(8,128)(2,1)S(1)}, bf16[80,1024]{1,0:T(8,128)(2,1)S(1)}, u32[]{:S(2)}, u32[]{:S(2)}) %collective-permute-start.25) | collective-permute-done | bytes 163872 | tf_op jit(solution)/shard_map/ppermute | solution.py:43
  102.2 5.2 %collective-permute-done.26.refs_4_ = bf16[80,1024]{1,0:T(8,128)(2,1)S(1)} collective-permute-done((bf16[80,1024]{1,0:T(8,128)(2,1)S(1)}, bf16[80,1024]{1,0:T(8,128)(2,1)S(1)}, u32[]{:S(2)}, u32[]{:S(2)}) %collective-permute-start.26) | collective-permute-done | bytes 163872 | tf_op jit(solution)/shard_map/ppermute | solution.py:43
  107.5 1.3 %shard_map.166 = bf16[2,1,128,1024]{3,2,1,0:T(8,128)(2,1)} custom-call(f32[128,1024]{1,0:T(8,128)S(1)} %get-tuple-element.47.refs_0_, f32[2,128]{1,0:T(2,128)S(1)} %get-tuple-element.48.refs_1_, s32[2,128]{1,0:T(2,128)S(1)} %get-tuple-element.49.refs_2_, bf16[80,1024]{1,0:T(8,128)(2,1)S(1)} %collective-permute-done.25.refs_3_, ...), custom_call_target="tpu_custom_call" | custom-call | flops 1 | bytes 1 | tf_op jit(solution)/shard_map/pallas_call | solution.py:450
  (41 shorter events, 0.2 us)
Async XLA Ops:
  0.0 12.6 %copy-start.5 = (bf16[2,1,128,1024]{3,2,1,0:T(8,128)(2,1)S(1)}, bf16[2,1,128,1024]{3,2,1,0:T(8,128)(2,1)}, u32[]{:S(2)}) copy-start(bf16[2,1,128,1024]{3,2,1,0:T(8,128)(2,1)} %refs_11_.4) | copy-start | bytes 1572868
  0.0 12.6 %copy-start.4 = (bf16[2,1,128,1024]{3,2,1,0:T(8,128)(2,1)S(1)}, bf16[2,1,128,1024]{3,2,1,0:T(8,128)(2,1)}, u32[]{:S(2)}) copy-start(bf16[2,1,128,1024]{3,2,1,0:T(8,128)(2,1)} %refs_3_.5) | copy-start | bytes 1572868
  1.2 19.0 %copy-start.8 = (f32[16,32]{1,0:T(8,128)S(1)}, f32[16,32]{1,0:T(8,128)}, u32[]{:S(2)}) copy-start(f32[16,32]{1,0:T(8,128)} %refs_0_.5) | copy-start | bytes 6148
  2.0 18.1 %copy-start.3 = (bf16[1024,1024]{1,0:T(8,128)(2,1)S(1)}, bf16[1024,1024]{1,0:T(8,128)(2,1)}, u32[]{:S(2)}) copy-start(bf16[1024,1024]{1,0:T(8,128)(2,1)} %refs_12_.2) | copy-start | bytes 6291460
  2.0 4.3 %collective-permute-start = (bf16[256,1024]{1,0:T(8,128)(2,1)}, bf16[256,1024]{1,0:T(8,128)(2,1)}, u32[]{:S(2)}, u32[]{:S(2)}) collective-permute-start(bf16[256,1024]{1,0:T(8,128)(2,1)} %shard_map.145.refs_2_.refs_3_), channel_id=1, source_target_pairs={{0,8},{8,0},{16,24},{24,16},{1,9},{9,1},{17,25},{25,17},{2,10},{10... | collective-permute-start | bytes 1572872 | tf_op jit(solution)/shard_map/ppermute | solution.py:43
  2.5 15.5 %collective-permute-start.2 = (bf16[256,1024]{1,0:T(8,128)(2,1)}, bf16[256,1024]{1,0:T(8,128)(2,1)}, u32[]{:S(2)}, u32[]{:S(2)}) collective-permute-start(bf16[256,1024]{1,0:T(8,128)(2,1)} %shard_map.145.refs_2_.refs_3_), channel_id=1, source_target_pairs={{0,16},{8,24},{16,0},{24,8},{1,17},{9,25},{17,1},{25,9},{2,18},{10... | collective-permute-start | bytes 1572872 | tf_op jit(solution)/shard_map/ppermute | solution.py:43
  6.4 5.0 %collective-permute-start.1 = (s32[2,128]{1,0:T(2,128)S(1)}, s32[2,128]{1,0:T(2,128)S(1)}, u32[]{:S(2)}, u32[]{:S(2)}) collective-permute-start(s32[2,128]{1,0:T(2,128)S(1)} %get-tuple-element.37.refs_0_), channel_id=1, source_target_pairs={{0,4},{1,5},{2,6},{3,7},{4,0},{5,1},{6,2},{7,3},{8,12},{9,13},{10,... | collective-permute-start | bytes 3080 | tf_op jit(solution)/shard_map/ppermute | solution.py:43
  9.0 3.2 %collective-permute-start.6 = (s32[2,128]{1,0:T(2,128)S(1)}, s32[2,128]{1,0:T(2,128)S(1)}, u32[]{:S(2)}, u32[]{:S(2)}) collective-permute-start(s32[2,128]{1,0:T(2,128)S(1)} %get-tuple-element.38), channel_id=1, source_target_pairs={{0,8},{8,0},{16,24},{24,16},{1,9},{9,1},{17,25},{25,17},{2,10},{10... | collective-permute-start | bytes 3080 | tf_op jit(solution)/shard_map/ppermute | solution.py:43
  9.0 8.9 %collective-permute-start.7 = (s32[2,128]{1,0:T(2,128)S(1)}, s32[2,128]{1,0:T(2,128)S(1)}, u32[]{:S(2)}, u32[]{:S(2)}) collective-permute-start(s32[2,128]{1,0:T(2,128)S(1)} %get-tuple-element.38), channel_id=1, source_target_pairs={{0,16},{8,24},{16,0},{24,8},{1,17},{9,25},{17,1},{25,9},{2,18},{10... | collective-permute-start | bytes 3080 | tf_op jit(solution)/shard_map/ppermute | solution.py:43
  9.8 8.1 %collective-permute-start.3 = (s32[2,128]{1,0:T(2,128)S(1)}, s32[2,128]{1,0:T(2,128)S(1)}, u32[]{:S(2)}, u32[]{:S(2)}) collective-permute-start(s32[2,128]{1,0:T(2,128)S(1)} %get-tuple-element.37.refs_0_), channel_id=1, source_target_pairs={{0,2},{1,3},{2,0},{3,1},{4,6},{5,7},{6,4},{7,5},{8,10},{9,11},{10,... | collective-permute-start | bytes 3080 | tf_op jit(solution)/shard_map/ppermute | solution.py:43
  11.4 6.5 %collective-permute-start.5 = (s32[2,128]{1,0:T(2,128)S(1)}, s32[2,128]{1,0:T(2,128)S(1)}, u32[]{:S(2)}, u32[]{:S(2)}) collective-permute-start(s32[2,128]{1,0:T(2,128)S(1)} %get-tuple-element.38), channel_id=1, source_target_pairs={{0,24},{8,16},{16,8},{24,0},{1,25},{9,17},{17,9},{25,1},{2,26},{10... | collective-permute-start | bytes 3080 | tf_op jit(solution)/shard_map/ppermute | solution.py:43
  12.2 5.7 %collective-permute-start.4 = (s32[2,128]{1,0:T(2,128)S(1)}, s32[2,128]{1,0:T(2,128)S(1)}, u32[]{:S(2)}, u32[]{:S(2)}) collective-permute-start(s32[2,128]{1,0:T(2,128)S(1)} %collective-permute-done.1.refs_4_.refs_2_), channel_id=1, source_target_pairs={{0,2},{1,3},{2,0},{3,1},{4,6},{5,7},{6,4},{7,5},{8,10},{9,11},{10,... | collective-permute-start | bytes 3080 | tf_op jit(solution)/shard_map/ppermute | solution.py:43
  12.6 1.0 copy-start.6
  13.7 1.0 copy-start.7
  17.9 2.2 %collective-permute-start.8 = (bf16[256,1024]{1,0:T(8,128)(2,1)}, bf16[256,1024]{1,0:T(8,128)(2,1)S(1)}, u32[]{:S(2)}, u32[]{:S(2)}) collective-permute-start(bf16[256,1024]{1,0:T(8,128)(2,1)} %shard_map.149.refs_5_.refs_12_), channel_id=1, source_target_pairs={{0,8},{8,0},{16,24},{24,16},{1,9},{9,1},{17,25},{25,17},{2,10},{10... | collective-permute-start | bytes 1572872 | tf_op jit(solution)/shard_map/ppermute | solution.py:43
  24.1 15.2 %collective-permute-start.13 = (bf16[128,1024]{1,0:T(8,128)(2,1)S(1)}, bf16[128,1024]{1,0:T(8,128)(2,1)S(1)}, u32[]{:S(2)}, u32[]{:S(2)}) collective-permute-start(bf16[128,1024]{1,0:T(8,128)(2,1)S(1)} %get-tuple-element.45.refs_5_.refs_3_), channel_id=1, source_target_pairs={{0,4},{1,5},{2,6},{3,7},{4,0},{5,1},{6,2},{7,3},{8,12},{9,13},{10,... | collective-permute-start | bytes 786440 | tf_op jit(solution)/shard_map/ppermute | solution.py:43
  27.0 12.9 %collective-permute-start.12 = (bf16[128,1024]{1,0:T(8,128)(2,1)S(1)}, bf16[128,1024]{1,0:T(8,128)(2,1)S(1)}, u32[]{:S(2)}, u32[]{:S(2)}) collective-permute-start(bf16[128,1024]{1,0:T(8,128)(2,1)S(1)} %get-tuple-element.45.refs_5_.refs_3_), channel_id=1, source_target_pairs={{0,2},{1,3},{2,0},{3,1},{4,6},{5,7},{6,4},{7,5},{8,10},{9,11},{10,... | collective-permute-start | bytes 786440 | tf_op jit(solution)/shard_map/ppermute | solution.py:43
  28.6 20.1 %collective-permute-start.10 = (bf16[256,1024]{1,0:T(8,128)(2,1)S(1)}, bf16[256,1024]{1,0:T(8,128)(2,1)S(1)}, u32[]{:S(2)}, u32[]{:S(2)}) collective-permute-start(bf16[256,1024]{1,0:T(8,128)(2,1)S(1)} %shard_map.151.refs_7_.refs_4_), channel_id=1, source_target_pairs={{0,16},{8,24},{16,0},{24,8},{1,17},{9,25},{17,1},{25,9},{2,18},{10... | collective-permute-start | bytes 1572872 | tf_op jit(solution)/shard_map/ppermute | solution.py:43
  30.1 18.6 %collective-permute-start.11 = (bf16[256,1024]{1,0:T(8,128)(2,1)S(1)}, bf16[256,1024]{1,0:T(8,128)(2,1)S(1)}, u32[]{:S(2)}, u32[]{:S(2)}) collective-permute-start(bf16[256,1024]{1,0:T(8,128)(2,1)S(1)} %shard_map.151.refs_7_.refs_4_), channel_id=1, source_target_pairs={{0,0},{8,16},{16,8},{24,24},{1,1},{9,17},{17,9},{25,25},{2,2},{10,... | collective-permute-start | bytes 1572872 | tf_op jit(solution)/shard_map/ppermute | solution.py:585
  30.9 17.8 %collective-permute-start.9 = (bf16[256,1024]{1,0:T(8,128)(2,1)S(1)}, bf16[256,1024]{1,0:T(8,128)(2,1)S(1)}, u32[]{:S(2)}, u32[]{:S(2)}) collective-permute-start(bf16[256,1024]{1,0:T(8,128)(2,1)S(1)} %shard_map.151.refs_7_.refs_4_), channel_id=1, source_target_pairs={{0,8},{8,0},{16,24},{24,16},{1,9},{9,1},{17,25},{25,17},{2,10},{10... | collective-permute-start | bytes 1572872 | tf_op jit(solution)/shard_map/ppermute | solution.py:43
  39.3 7.7 %collective-permute-start.14 = (bf16[128,1024]{1,0:T(8,128)(2,1)S(1)}, bf16[128,1024]{1,0:T(8,128)(2,1)S(1)}, u32[]{:S(2)}, u32[]{:S(2)}) collective-permute-start(bf16[128,1024]{1,0:T(8,128)(2,1)S(1)} %collective-permute-done.13.refs_1_.refs_5_), channel_id=1, source_target_pairs={{0,2},{1,3},{2,0},{3,1},{4,6},{5,7},{6,4},{7,5},{8,10},{9,11},{10,... | collective-permute-start | bytes 786440 | tf_op jit(solution)/shard_map/ppermute | solution.py:43
  39.9 8.8 %copy-start.9 = (bf16[1024,8]{0,1:T(8,128)(2,1)S(1)}, bf16[1024,8]{0,1:T(8,128)(2,1)}, u32[]{:S(2)}) copy-start(bf16[1024,8]{0,1:T(8,128)(2,1)} %param.22) | copy-start | bytes 49156
  39.9 17.3 %copy-start.2 = (bf16[1,1408,1024]{2,1,0:T(8,128)(2,1)S(1)}, bf16[1,1408,1024]{2,1,0:T(8,128)(2,1)}, u32[]{:S(2)}) copy-start(bf16[1,1408,1024]{2,1,0:T(8,128)(2,1)} %refs_3_.7) | copy-start | bytes 8650756
  40.4 16.9 %collective-permute-start.18 = (bf16[160,1024]{1,0:T(8,128)(2,1)S(1)}, bf16[160,1024]{1,0:T(8,128)(2,1)S(1)}, u32[]{:S(2)}, u32[]{:S(2)}) collective-permute-start(bf16[160,1024]{1,0:T(8,128)(2,1)S(1)} %get-tuple-element.54), channel_id=1, source_target_pairs={{0,1},{1,0},{2,3},{3,2},{4,5},{5,4},{6,7},{7,6},{8,9},{9,8},{10,11... | collective-permute-start | bytes 983048 | tf_op jit(solution)/shard_map/ppermute | solution.py:43
  47.0 10.3 %copy-start.1 = (bf16[1,1024,1408]{2,1,0:T(8,128)(2,1)S(1)}, bf16[1,1024,1408]{2,1,0:T(8,128)(2,1)}, u32[]{:S(2)}) copy-start(bf16[1,1024,1408]{2,1,0:T(8,128)(2,1)} %refs_2_.7) | copy-start | bytes 8650756
  47.3 10.0 %copy-start = (bf16[1,1024,1408]{2,1,0:T(8,128)(2,1)S(1)}, bf16[1,1024,1408]{2,1,0:T(8,128)(2,1)}, u32[]{:S(2)}) copy-start(bf16[1,1024,1408]{2,1,0:T(8,128)(2,1)} %refs_1_.3) | copy-start | bytes 8650756
  47.3 10.0 %collective-permute-start.19 = (bf16[160,1024]{1,0:T(8,128)(2,1)S(1)}, bf16[160,1024]{1,0:T(8,128)(2,1)S(1)}, u32[]{:S(2)}, u32[]{:S(2)}) collective-permute-start(bf16[160,1024]{1,0:T(8,128)(2,1)S(1)} %shard_map.153.refs_13_), channel_id=1, source_target_pairs={{0,1},{1,0},{2,3},{3,2},{4,5},{5,4},{6,7},{7,6},{8,9},{9,8},{10,11... | collective-permute-start | bytes 983048 | tf_op jit(solution)/shard_map/ppermute | solution.py:43
  52.4 13.3 %collective-permute-start.15 = (bf16[80,1024]{1,0:T(8,128)(2,1)S(1)}, bf16[80,1024]{1,0:T(8,128)(2,1)S(1)}, u32[]{:S(2)}, u32[]{:S(2)}) collective-permute-start(bf16[80,1024]{1,0:T(8,128)(2,1)S(1)} %get-tuple-element.50), channel_id=1, source_target_pairs={{0,6},{1,7},{2,4},{3,5},{4,2},{5,3},{6,0},{7,1},{8,14},{9,15},{10,... | collective-permute-start | bytes 491528 | tf_op jit(solution)/shard_map/ppermute | solution.py:43
  56.6 12.9 %collective-permute-start.16 = (bf16[80,1024]{1,0:T(8,128)(2,1)S(1)}, bf16[80,1024]{1,0:T(8,128)(2,1)S(1)}, u32[]{:S(2)}, u32[]{:S(2)}) collective-permute-start(bf16[80,1024]{1,0:T(8,128)(2,1)S(1)} %get-tuple-element.51), channel_id=1, source_target_pairs={{0,4},{1,5},{2,6},{3,7},{4,0},{5,1},{6,2},{7,3},{8,12},{9,13},{10,... | collective-permute-start | bytes 491528 | tf_op jit(solution)/shard_map/ppermute | solution.py:43
  56.6 12.9 %collective-permute-start.17 = (bf16[80,1024]{1,0:T(8,128)(2,1)S(1)}, bf16[80,1024]{1,0:T(8,128)(2,1)S(1)}, u32[]{:S(2)}, u32[]{:S(2)}) collective-permute-start(bf16[80,1024]{1,0:T(8,128)(2,1)S(1)} %get-tuple-element.52), channel_id=1, source_target_pairs={{0,2},{1,3},{2,0},{3,1},{4,6},{5,7},{6,4},{7,5},{8,10},{9,11},{10,... | collective-permute-start | bytes 491528 | tf_op jit(solution)/shard_map/ppermute | solution.py:43
  60.6 9.5 %collective-permute-start.20 = (bf16[160,1024]{1,0:T(8,128)(2,1)S(1)}, bf16[160,1024]{1,0:T(8,128)(2,1)S(1)}, u32[]{:S(2)}, u32[]{:S(2)}) collective-permute-start(bf16[160,1024]{1,0:T(8,128)(2,1)S(1)} %get-tuple-element.58), channel_id=1, source_target_pairs={{0,1},{1,0},{2,3},{3,2},{4,5},{5,4},{6,7},{7,6},{8,9},{9,8},{10,11... | collective-permute-start | bytes 983048 | tf_op jit(solution)/shard_map/ppermute | solution.py:43
  69.6 8.8 %collective-permute-start.21 = (bf16[160,1024]{1,0:T(8,128)(2,1)S(1)}, bf16[160,1024]{1,0:T(8,128)(2,1)S(1)}, u32[]{:S(2)}, u32[]{:S(2)}) collective-permute-start(bf16[160,1024]{1,0:T(8,128)(2,1)S(1)} %shard_map.157.refs_4_), channel_id=1, source_target_pairs={{0,1},{1,0},{2,3},{3,2},{4,5},{5,4},{6,7},{7,6},{8,9},{9,8},{10,11... | collective-permute-start | bytes 983048 | tf_op jit(solution)/shard_map/ppermute | solution.py:43
  70.9 11.4 %collective-permute-start.24 = (bf16[128,1024]{1,0:T(8,128)(2,1)S(1)}, bf16[128,1024]{1,0:T(8,128)(2,1)S(1)}, u32[]{:S(2)}, u32[]{:S(2)}) collective-permute-start(bf16[128,1024]{1,0:T(8,128)(2,1)S(1)} %get-tuple-element.60), channel_id=1, source_target_pairs={{0,2},{1,3},{2,0},{3,1},{4,6},{5,7},{6,4},{7,5},{8,10},{9,11},{10,... | collective-permute-start | bytes 786440 | tf_op jit(solution)/shard_map/ppermute | solution.py:43
  78.4 10.6 %collective-permute-start.23 = (bf16[160,1024]{1,0:T(8,128)(2,1)S(1)}, bf16[160,1024]{1,0:T(8,128)(2,1)S(1)}, u32[]{:S(2)}, u32[]{:S(2)}) collective-permute-start(bf16[160,1024]{1,0:T(8,128)(2,1)S(1)} %shard_map.160.refs_4_), channel_id=1, source_target_pairs={{0,1},{1,0},{2,3},{3,2},{4,5},{5,4},{6,7},{7,6},{8,9},{9,8},{10,11... | collective-permute-start | bytes 983048 | tf_op jit(solution)/shard_map/ppermute | solution.py:43
  80.5 12.7 %collective-permute-start.22 = (bf16[160,1024]{1,0:T(8,128)(2,1)S(1)}, bf16[160,1024]{1,0:T(8,128)(2,1)S(1)}, u32[]{:S(2)}, u32[]{:S(2)}) collective-permute-start(bf16[160,1024]{1,0:T(8,128)(2,1)S(1)} %shard_map.161.refs_2_), channel_id=1, source_target_pairs={{0,1},{1,0},{2,3},{3,2},{4,5},{5,4},{6,7},{7,6},{8,9},{9,8},{10,11... | collective-permute-start | bytes 983048 | tf_op jit(solution)/shard_map/ppermute | solution.py:43
  82.3 15.4 %collective-permute-start.28 = (bf16[128,1024]{1,0:T(8,128)(2,1)S(1)}, bf16[128,1024]{1,0:T(8,128)(2,1)S(1)}, u32[]{:S(2)}, u32[]{:S(2)}) collective-permute-start(bf16[128,1024]{1,0:T(8,128)(2,1)S(1)} %shard_map.162.refs_4_), channel_id=1, source_target_pairs={{0,4},{1,5},{2,6},{3,7},{4,0},{5,1},{6,2},{7,3},{8,12},{9,13},{10,... | collective-permute-start | bytes 786440 | tf_op jit(solution)/shard_map/ppermute | solution.py:43
  89.8 17.7 %collective-permute-start.29 = (bf16[128,1024]{1,0:T(8,128)(2,1)S(1)}, bf16[128,1024]{1,0:T(8,128)(2,1)S(1)}, u32[]{:S(2)}, u32[]{:S(2)}) collective-permute-start(bf16[128,1024]{1,0:T(8,128)(2,1)S(1)} %get-tuple-element.66), channel_id=1, source_target_pairs={{0,2},{1,3},{2,0},{3,1},{4,6},{5,7},{6,4},{7,5},{8,10},{9,11},{10,... | collective-permute-start | bytes 786440 | tf_op jit(solution)/shard_map/ppermute | solution.py:43
  93.2 9.0 %collective-permute-start.25 = (bf16[80,1024]{1,0:T(8,128)(2,1)S(1)}, bf16[80,1024]{1,0:T(8,128)(2,1)S(1)}, u32[]{:S(2)}, u32[]{:S(2)}) collective-permute-start(bf16[80,1024]{1,0:T(8,128)(2,1)S(1)} %get-tuple-element.62), channel_id=1, source_target_pairs={{0,6},{1,7},{2,4},{3,5},{4,2},{5,3},{6,0},{7,1},{8,14},{9,15},{10,... | collective-permute-start | bytes 491528 | tf_op jit(solution)/shard_map/ppermute | solution.py:43
  94.1 13.4 %collective-permute-start.26 = (bf16[80,1024]{1,0:T(8,128)(2,1)S(1)}, bf16[80,1024]{1,0:T(8,128)(2,1)S(1)}, u32[]{:S(2)}, u32[]{:S(2)}) collective-permute-start(bf16[80,1024]{1,0:T(8,128)(2,1)S(1)} %get-tuple-element.63), channel_id=1, source_target_pairs={{0,4},{1,5},{2,6},{3,7},{4,0},{5,1},{6,2},{7,3},{8,12},{9,13},{10,... | collective-permute-start | bytes 491528 | tf_op jit(solution)/shard_map/ppermute | solution.py:43
  94.9 12.6 %collective-permute-start.27 = (bf16[80,1024]{1,0:T(8,128)(2,1)S(1)}, bf16[80,1024]{1,0:T(8,128)(2,1)S(1)}, u32[]{:S(2)}, u32[]{:S(2)}) collective-permute-start(bf16[80,1024]{1,0:T(8,128)(2,1)S(1)} %get-tuple-element.64), channel_id=1, source_target_pairs={{0,2},{1,3},{2,0},{3,1},{4,6},{5,7},{6,4},{7,5},{8,10},{9,11},{10,... | collective-permute-start | bytes 491528 | tf_op jit(solution)/shard_map/ppermute | solution.py:43

commit v2 on v1

--- a/solution.py
+++ b/solution.py
@@ -629,12 +629,12 @@
         after=[crossed_one],
     )
     low_far = swapped(low_out, "exp", 1)
+    send_down(m for m in upper if m % 2 == 0)
     far_one = call(
         direct_far_kernel, shaped((half_one, width), bf16), [VMEM] * 4, (crossed_one, *weights),
         scratch=scratch_for(half_one)[1:],
     )
     far_one = swapped(far_one, "exp", 1)
-    send_down(m for m in upper if m % 2 == 0)
     partial(lower, low_far)
     send_down(m for m in lower if m)
     answers = call(rejoin_kernel, [packet] * columns, [VMEM] * 2, (near_one, far_one))

time: 109 us -> 110 us (level)
  starting transfers between devices: 36.2 us -> 37.6 us
    ppermute x29, starting transfers between devices: 35.3 us -> 36.8 us  [swapped(): lax.ppermute(value, axis, [(source, source ^ mask) for source in range(co...]
  transfers between devices with their start and end apart: 30 -> 30, of which waited for: 10 -> 10; matrix products, arithmetic and copies ran while one was open for 1% -> 1% of each run, Pallas kernels for 16% -> 15%
where the time goes in v2:
time: 110 us; the launch traced here: 109 us
  waiting for transfers between devices  43.7 us (40%)
  starting transfers between devices  37.6 us (34%)
  Pallas kernels  23 us (21%)
  local copies, waits for them, and re-layouts  4.67 us (4%)
    ppermute x29, waiting for transfers between devices, swapped(): lax.ppermute(value, axis, [(source, source ^ mask) for source in range(co...  43.7 us
    ppermute x29, starting transfers between devices, swapped(): lax.ppermute(value, axis, [(source, source ^ mask) for source in range(co...  36.8 us
    pallas_call x22, Pallas kernels, call(): pl.pallas_call(body, out_shape=outs, in_specs=ins + [ANY] * len(after), o...  23 us
  transfers between devices with their start and end apart: 30, of which 10 were waited for; matrix products, arithmetic and copies ran while one was open for 1% of the time, Pallas kernels for 15%

profile of v2, /device:TPU:0, one launch (start us, length us, event | category | flops | bytes accessed | tf_op | source)
XLA Modules:
  0.0 109.3 jit_solution(10767490705791745312)
XLA Ops:
  0.0 1.2 %slice_bitcast_fusion = (bf16[128,1024]{1,0:T(8,128)(2,1)S(1)}, bf16[128,1024]{1,0:T(8,128)(2,1)S(1)}) fusion(bf16[2,1,128,1024]{3,2,1,0:T(8,128)(2,1)} %refs_1_.2, bf16[2,1,128,1024]{3,2,1,0:T(8,128)(2,1)} %refs_0_.3), kind=kLoop, calls=%fused_computation | loop fusion | bytes 1048576 | tf_op jit(solution)/shard_map/squeeze | solution.py:540
  1.2 0.0 copy-start.8
  1.2 0.8 shard_map.145.refs_2_.refs_3_
  2.0 0.5 collective-permute-start
  2.5 2.5 %collective-permute-start.2 = (bf16[256,1024]{1,0:T(8,128)(2,1)}, bf16[256,1024]{1,0:T(8,128)(2,1)}, u32[]{:S(2)}, u32[]{:S(2)}) collective-permute-start(bf16[256,1024]{1,0:T(8,128)(2,1)} %shard_map.145.refs_2_.refs_3_), channel_id=1, source_target_pairs={{0,16},{8,24},{16,0},{24,8},{1,17},{9,25},{17,1},{25,9},{2,18},{10... | collective-permute-start | bytes 1572872 | tf_op jit(solution)/shard_map/ppermute | solution.py:43
  4.9 0.7 pad_bitcast_fusion
  5.6 0.7 concatenate.3.refs_0_
  6.3 0.0 collective-permute-done.refs_1_.refs_4_
  6.4 2.7 %collective-permute-start.1 = (s32[2,128]{1,0:T(2,128)S(1)}, s32[2,128]{1,0:T(2,128)S(1)}, u32[]{:S(2)}, u32[]{:S(2)}) collective-permute-start(s32[2,128]{1,0:T(2,128)S(1)} %get-tuple-element.37.refs_0_), channel_id=1, source_target_pairs={{0,4},{1,5},{2,6},{3,7},{4,0},{5,1},{6,2},{7,3},{8,12},{9,13},{10,... | collective-permute-start | bytes 3080 | tf_op jit(solution)/shard_map/ppermute | solution.py:43
  9.0 0.8 collective-permute-start.7
  9.8 1.6 %collective-permute-start.3 = (s32[2,128]{1,0:T(2,128)S(1)}, s32[2,128]{1,0:T(2,128)S(1)}, u32[]{:S(2)}, u32[]{:S(2)}) collective-permute-start(s32[2,128]{1,0:T(2,128)S(1)} %get-tuple-element.37.refs_0_), channel_id=1, source_target_pairs={{0,2},{1,3},{2,0},{3,1},{4,6},{5,7},{6,4},{7,5},{8,10},{9,11},{10,... | collective-permute-start | bytes 3080 | tf_op jit(solution)/shard_map/ppermute | solution.py:43
  11.4 0.8 collective-permute-start.5
  12.2 0.0 collective-permute-done.6.refs_5_.refs_7_.refs_8_
  12.2 0.5 collective-permute-start.4
  12.6 1.0 copy-done.6
  13.7 1.0 copy-done.7
  14.8 3.1 %collective-permute-done.7.refs_6_.refs_8_.refs_9_ = s32[2,128]{1,0:T(2,128)S(1)} collective-permute-done((s32[2,128]{1,0:T(2,128)S(1)}, s32[2,128]{1,0:T(2,128)S(1)}, u32[]{:S(2)}, u32[]{:S(2)}) %collective-permute-start.7) | collective-permute-done | bytes 1056 | tf_op jit(solution)/shard_map/ppermute | solution.py:43
  17.9 0.0 collective-permute-done.3.refs_1_
  17.9 0.0 collective-permute-done.2.refs_0_
  17.9 0.2 collective-permute-start.8
  18.1 2.0 %collective-permute-done.8.refs_6_ = bf16[256,1024]{1,0:T(8,128)(2,1)S(1)} collective-permute-done((bf16[256,1024]{1,0:T(8,128)(2,1)}, bf16[256,1024]{1,0:T(8,128)(2,1)S(1)}, u32[]{:S(2)}, u32[]{:S(2)}) %collective-permute-start.8) | collective-permute-done | bytes 524320 | tf_op jit(solution)/shard_map/ppermute | solution.py:43
  20.1 4.0 %shard_map.150 = (f32[128,1024]{1,0:T(8,128)S(1)}, bf16[128,1024]{1,0:T(8,128)(2,1)S(1)}) custom-call(f32[16,32]{1,0:T(8,128)S(1)} %copy-done.8, s32[8,128]{1,0:T(8,128)S(1)} %get-tuple-element.36.refs_5_.refs_1_.refs_0_.refs_2_, bf16[2,1,128,1024]{3,2,1,0:T(8,128)(2,1)S(1)} %copy-done.4, bf16[256,1024]{1,0:T(8,128)(2,1)} %shard_map.145.refs_2_.refs_3_, ...), custom_call_target="tpu_custom_call" | custom-call | flops 1 | bytes 1 | tf_op jit(solution)/shard_map/pallas_call | solution.py:450
  24.1 2.9 %collective-permute-start.13 = (bf16[128,1024]{1,0:T(8,128)(2,1)S(1)}, bf16[128,1024]{1,0:T(8,128)(2,1)S(1)}, u32[]{:S(2)}, u32[]{:S(2)}) collective-permute-start(bf16[128,1024]{1,0:T(8,128)(2,1)S(1)} %get-tuple-element.45.refs_5_.refs_3_), channel_id=1, source_target_pairs={{0,4},{1,5},{2,6},{3,7},{4,0},{5,1},{6,2},{7,3},{8,12},{9,13},{10,... | collective-permute-start | bytes 786440 | tf_op jit(solution)/shard_map/ppermute | solution.py:43
  27.0 1.6 %collective-permute-start.12 = (bf16[128,1024]{1,0:T(8,128)(2,1)S(1)}, bf16[128,1024]{1,0:T(8,128)(2,1)S(1)}, u32[]{:S(2)}, u32[]{:S(2)}) collective-permute-start(bf16[128,1024]{1,0:T(8,128)(2,1)S(1)} %get-tuple-element.45.refs_5_.refs_3_), channel_id=1, source_target_pairs={{0,2},{1,3},{2,0},{3,1},{4,6},{5,7},{6,4},{7,5},{8,10},{9,11},{10,... | collective-permute-start | bytes 786440 | tf_op jit(solution)/shard_map/ppermute | solution.py:43
  28.6 1.5 %collective-permute-start.10 = (bf16[256,1024]{1,0:T(8,128)(2,1)S(1)}, bf16[256,1024]{1,0:T(8,128)(2,1)S(1)}, u32[]{:S(2)}, u32[]{:S(2)}) collective-permute-start(bf16[256,1024]{1,0:T(8,128)(2,1)S(1)} %shard_map.151.refs_7_.refs_4_), channel_id=1, source_target_pairs={{0,16},{8,24},{16,0},{24,8},{1,17},{9,25},{17,1},{25,9},{2,18},{10... | collective-permute-start | bytes 1572872 | tf_op jit(solution)/shard_map/ppermute | solution.py:43
  30.1 0.9 collective-permute-start.11
  30.9 1.9 %collective-permute-start.9 = (bf16[256,1024]{1,0:T(8,128)(2,1)S(1)}, bf16[256,1024]{1,0:T(8,128)(2,1)S(1)}, u32[]{:S(2)}, u32[]{:S(2)}) collective-permute-start(bf16[256,1024]{1,0:T(8,128)(2,1)S(1)} %shard_map.151.refs_7_.refs_4_), channel_id=1, source_target_pairs={{0,8},{8,0},{16,24},{24,16},{1,9},{9,1},{17,25},{25,17},{2,10},{10... | collective-permute-start | bytes 1572872 | tf_op jit(solution)/shard_map/ppermute | solution.py:43
  32.9 6.5 %collective-permute-done.13.refs_1_.refs_5_ = bf16[128,1024]{1,0:T(8,128)(2,1)S(1)} collective-permute-done((bf16[128,1024]{1,0:T(8,128)(2,1)S(1)}, bf16[128,1024]{1,0:T(8,128)(2,1)S(1)}, u32[]{:S(2)}, u32[]{:S(2)}) %collective-permute-start.13) | collective-permute-done | bytes 262176 | tf_op jit(solution)/shard_map/ppermute | solution.py:43
  39.3 0.6 collective-permute-start.14
  39.9 0.0 collective-permute-done.12.refs_6_.refs_4_
  39.9 0.5 shard_map.152
  40.4 1.6 %collective-permute-start.18 = (bf16[160,1024]{1,0:T(8,128)(2,1)S(1)}, bf16[160,1024]{1,0:T(8,128)(2,1)S(1)}, u32[]{:S(2)}, u32[]{:S(2)}) collective-permute-start(bf16[160,1024]{1,0:T(8,128)(2,1)S(1)} %get-tuple-element.54), channel_id=1, source_target_pairs={{0,1},{1,0},{2,3},{3,2},{4,5},{5,4},{6,7},{7,6},{8,9},{9,8},{10,11... | collective-permute-start | bytes 983048 | tf_op jit(solution)/shard_map/ppermute | solution.py:43
  42.0 5.0 %collective-permute-done.14.refs_2_.refs_6_ = bf16[128,1024]{1,0:T(8,128)(2,1)S(1)} collective-permute-done((bf16[128,1024]{1,0:T(8,128)(2,1)S(1)}, bf16[128,1024]{1,0:T(8,128)(2,1)S(1)}, u32[]{:S(2)}, u32[]{:S(2)}) %collective-permute-start.14) | collective-permute-done | bytes 262176 | tf_op jit(solution)/shard_map/ppermute | solution.py:43
  47.0 0.2 shard_map.153.refs_13_
  47.3 0.0 copy-start
  47.3 1.4 %collective-permute-start.19 = (bf16[160,1024]{1,0:T(8,128)(2,1)S(1)}, bf16[160,1024]{1,0:T(8,128)(2,1)S(1)}, u32[]{:S(2)}, u32[]{:S(2)}) collective-permute-start(bf16[160,1024]{1,0:T(8,128)(2,1)S(1)} %shard_map.153.refs_13_), channel_id=1, source_target_pairs={{0,1},{1,0},{2,3},{3,2},{4,5},{5,4},{6,7},{7,6},{8,9},{9,8},{10,11... | collective-permute-start | bytes 983048 | tf_op jit(solution)/shard_map/ppermute | solution.py:43
  48.7 3.7 %shard_map.154 = (bf16[80,1024]{1,0:T(8,128)(2,1)S(1)}, bf16[80,1024]{1,0:T(8,128)(2,1)S(1)}, bf16[80,1024]{1,0:T(8,128)(2,1)S(1)}, bf16[80,1024]{1,0:T(8,128)(2...) custom-call(f32[16,32]{1,0:T(8,128)S(1)} %copy-done.8, ...), custom_call_target="tpu_custom_call" | custom-call | flops 1 | bytes 1 | tf_op jit(solution)/shard_map/pallas_call | solution.py:450
  52.4 4.2 %collective-permute-start.15 = (bf16[80,1024]{1,0:T(8,128)(2,1)S(1)}, bf16[80,1024]{1,0:T(8,128)(2,1)S(1)}, u32[]{:S(2)}, u32[]{:S(2)}) collective-permute-start(bf16[80,1024]{1,0:T(8,128)(2,1)S(1)} %get-tuple-element.50), channel_id=1, source_target_pairs={{0,6},{1,7},{2,4},{3,5},{4,2},{5,3},{6,0},{7,1},{8,14},{9,15},{10,... | collective-permute-start | bytes 491528 | tf_op jit(solution)/shard_map/ppermute | solution.py:43
  56.6 0.6 collective-permute-start.17
  57.3 3.3 %shard_map.155 = (bf16[160,1024]{1,0:T(8,128)(2,1)S(1)}, bf16[160,1024]{1,0:T(8,128)(2,1)S(1)}) custom-call(bf16[160,1024]{1,0:T(8,128)(2,1)S(1)} %collective-permute-done.18.refs_0_, bf16[160,1024]{1,0:T(8,128)(2,1)S(1)} %collective-permute-done.19.refs_1_, bf16[1,1024,1408]{2,1,0:T(8,128)(2,1)S(1)} %copy-done, bf16[1,1024,1408]{2,1,0:T(8,128)(2,1)S(1)} %copy-done.1, ...), custom_call_target="tpu_custom_call" | custom-call | flops 1 | bytes 1 | tf_op jit(solution)/shard_map/pallas_call | solution.py:450
  60.6 1.2 %collective-permute-start.20 = (bf16[160,1024]{1,0:T(8,128)(2,1)S(1)}, bf16[160,1024]{1,0:T(8,128)(2,1)S(1)}, u32[]{:S(2)}, u32[]{:S(2)}) collective-permute-start(bf16[160,1024]{1,0:T(8,128)(2,1)S(1)} %get-tuple-element.58), channel_id=1, source_target_pairs={{0,1},{1,0},{2,3},{3,2},{4,5},{5,4},{6,7},{7,6},{8,9},{9,8},{10,11... | collective-permute-start | bytes 983048 | tf_op jit(solution)/shard_map/ppermute | solution.py:43
  61.8 3.9 %shard_map.156 = (bf16[320,1024]{1,0:T(8,128)(2,1)S(1)}, f32[8,128]{1,0:T(8,128)S(1)}) custom-call(s32[8,128]{1,0:T(8,128)S(1)} %get-tuple-element.36.refs_5_.refs_1_.refs_0_.refs_2_, s32[8,128]{1,0:T(8,128)S(1)} %get-tuple-element.46.refs_0_.refs_3_.refs_1_, bf16[8,1024]{1,0:T(8,128)(2,1)S(1)} %bitcast.17, ...), custom_call_target="tpu_custom_call" | custom-call | flops 4000000000 | bytes 1 | tf_op jit(solution)/shard_map/pallas_call | solution.py:450
  65.7 3.9 %collective-permute-done.16.refs_1_ = bf16[80,1024]{1,0:T(8,128)(2,1)S(1)} collective-permute-done((bf16[80,1024]{1,0:T(8,128)(2,1)S(1)}, bf16[80,1024]{1,0:T(8,128)(2,1)S(1)}, u32[]{:S(2)}, u32[]{:S(2)}) %collective-permute-start.16) | collective-permute-done | bytes 163872 | tf_op jit(solution)/shard_map/ppermute | solution.py:43
  69.6 0.6 collective-permute-start.21
  70.2 0.7 shard_map.158
  70.9 0.1 collective-permute-start.22
  71.0 1.8 %shard_map.159.refs_2_.refs_0_ = bf16[160,1024]{1,0:T(8,128)(2,1)S(1)} custom-call(bf16[80,1024]{1,0:T(8,128)(2,1)S(1)} %collective-permute-done.15.refs_0_, bf16[80,1024]{1,0:T(8,128)(2,1)S(1)} %collective-permute-done.16.refs_1_, bf16[80,1024]{1,0:T(8,128)(2,1)S(1)} %collective-permute-done.17.refs_2_, ...), custom_call_target="tpu_custom_call" | custom-call | flops 1 | bytes 1 | tf_op jit(solution)/shard_map/pallas_call | solution.py:450
  72.8 5.6 %collective-permute-done.21.refs_1_.refs_0_ = bf16[160,1024]{1,0:T(8,128)(2,1)S(1)} collective-permute-done((bf16[160,1024]{1,0:T(8,128)(2,1)S(1)}, bf16[160,1024]{1,0:T(8,128)(2,1)S(1)}, u32[]{:S(2)}, u32[]{:S(2)}) %collective-permute-start.21) | collective-permute-done | bytes 327712 | tf_op jit(solution)/shard_map/ppermute | solution.py:43
  78.4 0.3 collective-permute-start.24
  78.7 1.8 %shard_map.162.refs_4_ = bf16[160,1024]{1,0:T(8,128)(2,1)S(1)} custom-call(bf16[160,1024]{1,0:T(8,128)(2,1)S(1)} %collective-permute-done.21.refs_1_.refs_0_, bf16[1,1024,1408]{2,1,0:T(8,128)(2,1)S(1)} %copy-done, bf16[1,1024,1408]{2,1,0:T(8,128)(2,1)S(1)} %copy-done.1, bf16[1,1408,1024]{2,1,0:T(8,128)(2,1)S(1)} %copy-done.2, ...), custom_call_target="tpu_custom_call" | custom-call | flops 1 | bytes 1 | tf_op jit(solution)/shard_map/pallas_call | solution.py:450
  80.5 1.8 %collective-permute-start.23 = (bf16[160,1024]{1,0:T(8,128)(2,1)S(1)}, bf16[160,1024]{1,0:T(8,128)(2,1)S(1)}, u32[]{:S(2)}, u32[]{:S(2)}) collective-permute-start(bf16[160,1024]{1,0:T(8,128)(2,1)S(1)} %shard_map.162.refs_4_), channel_id=1, source_target_pairs={{0,1},{1,0},{2,3},{3,2},{4,5},{5,4},{6,7},{7,6},{8,9},{9,8},{10,11... | collective-permute-start | bytes 983048 | tf_op jit(solution)/shard_map/ppermute | solution.py:43
  82.3 2.6 %collective-permute-start.28 = (bf16[128,1024]{1,0:T(8,128)(2,1)S(1)}, bf16[128,1024]{1,0:T(8,128)(2,1)S(1)}, u32[]{:S(2)}, u32[]{:S(2)}) collective-permute-start(bf16[128,1024]{1,0:T(8,128)(2,1)S(1)} %shard_map.161.refs_4_), channel_id=1, source_target_pairs={{0,4},{1,5},{2,6},{3,7},{4,0},{5,1},{6,2},{7,3},{8,12},{9,13},{10,... | collective-permute-start | bytes 786440 | tf_op jit(solution)/shard_map/ppermute | solution.py:43
  84.9 4.1 %collective-permute-done.24.refs_3_ = bf16[160,1024]{1,0:T(8,128)(2,1)S(1)} collective-permute-done((bf16[160,1024]{1,0:T(8,128)(2,1)S(1)}, bf16[160,1024]{1,0:T(8,128)(2,1)S(1)}, u32[]{:S(2)}, u32[]{:S(2)}) %collective-permute-start.24) | collective-permute-done | bytes 327712 | tf_op jit(solution)/shard_map/ppermute | solution.py:43
  89.0 0.7 shard_map.163
  89.8 0.1 collective-permute-start.29
  89.9 3.3 %collective-permute-done.23.refs_1_ = bf16[160,1024]{1,0:T(8,128)(2,1)S(1)} collective-permute-done((bf16[160,1024]{1,0:T(8,128)(2,1)S(1)}, bf16[160,1024]{1,0:T(8,128)(2,1)S(1)}, u32[]{:S(2)}, u32[]{:S(2)}) %collective-permute-start.23) | collective-permute-done | bytes 327712 | tf_op jit(solution)/shard_map/ppermute | solution.py:43
  93.2 0.9 collective-permute-start.25
  94.1 0.8 collective-permute-start.26
  94.9 2.8 %collective-permute-start.27 = (bf16[80,1024]{1,0:T(8,128)(2,1)S(1)}, bf16[80,1024]{1,0:T(8,128)(2,1)S(1)}, u32[]{:S(2)}, u32[]{:S(2)}) collective-permute-start(bf16[80,1024]{1,0:T(8,128)(2,1)S(1)} %get-tuple-element.64), channel_id=1, source_target_pairs={{0,2},{1,3},{2,0},{3,1},{4,6},{5,7},{6,4},{7,5},{8,10},{9,11},{10,... | collective-permute-start | bytes 491528 | tf_op jit(solution)/shard_map/ppermute | solution.py:43
  97.7 0.1 shard_map.165.refs_7_.refs_10_
  97.8 6.1 %collective-permute-done.29.refs_9_ = bf16[128,1024]{1,0:T(8,128)(2,1)S(1)} collective-permute-done((bf16[128,1024]{1,0:T(8,128)(2,1)S(1)}, bf16[128,1024]{1,0:T(8,128)(2,1)S(1)}, u32[]{:S(2)}, u32[]{:S(2)}) %collective-permute-start.29) | collective-permute-done | bytes 262176 | tf_op jit(solution)/shard_map/ppermute | solution.py:43
  103.9 4.1 %collective-permute-done.26.refs_4_ = bf16[80,1024]{1,0:T(8,128)(2,1)S(1)} collective-permute-done((bf16[80,1024]{1,0:T(8,128)(2,1)S(1)}, bf16[80,1024]{1,0:T(8,128)(2,1)S(1)}, u32[]{:S(2)}, u32[]{:S(2)}) %collective-permute-start.26) | collective-permute-done | bytes 163872 | tf_op jit(solution)/shard_map/ppermute | solution.py:43
  107.9 0.0 collective-permute-done.27.refs_5_
  107.9 1.4 %shard_map.166 = bf16[2,1,128,1024]{3,2,1,0:T(8,128)(2,1)} custom-call(f32[128,1024]{1,0:T(8,128)S(1)} %get-tuple-element.47.refs_0_, f32[2,128]{1,0:T(2,128)S(1)} %get-tuple-element.48.refs_1_, s32[2,128]{1,0:T(2,128)S(1)} %get-tuple-element.49.refs_2_, bf16[80,1024]{1,0:T(8,128)(2,1)S(1)} %collective-permute-done.25.refs_3_, ...), custom_call_target="tpu_custom_call" | custom-call | flops 1 | bytes 1 | tf_op jit(solution)/shard_map/pallas_call | solution.py:450
  (41 shorter events, 0.2 us)
Async XLA Ops:
  0.0 12.6 %copy-start.5 = (bf16[2,1,128,1024]{3,2,1,0:T(8,128)(2,1)S(1)}, bf16[2,1,128,1024]{3,2,1,0:T(8,128)(2,1)}, u32[]{:S(2)}) copy-start(bf16[2,1,128,1024]{3,2,1,0:T(8,128)(2,1)} %refs_11_.4) | copy-start | bytes 1572868
  0.0 12.6 %copy-start.4 = (bf16[2,1,128,1024]{3,2,1,0:T(8,128)(2,1)S(1)}, bf16[2,1,128,1024]{3,2,1,0:T(8,128)(2,1)}, u32[]{:S(2)}) copy-start(bf16[2,1,128,1024]{3,2,1,0:T(8,128)(2,1)} %refs_3_.5) | copy-start | bytes 1572868
  1.2 19.0 %copy-start.8 = (f32[16,32]{1,0:T(8,128)S(1)}, f32[16,32]{1,0:T(8,128)}, u32[]{:S(2)}) copy-start(f32[16,32]{1,0:T(8,128)} %refs_0_.5) | copy-start | bytes 6148
  2.0 18.1 %copy-start.3 = (bf16[1024,1024]{1,0:T(8,128)(2,1)S(1)}, bf16[1024,1024]{1,0:T(8,128)(2,1)}, u32[]{:S(2)}) copy-start(bf16[1024,1024]{1,0:T(8,128)(2,1)} %refs_12_.2) | copy-start | bytes 6291460
  2.0 4.3 %collective-permute-start = (bf16[256,1024]{1,0:T(8,128)(2,1)}, bf16[256,1024]{1,0:T(8,128)(2,1)}, u32[]{:S(2)}, u32[]{:S(2)}) collective-permute-start(bf16[256,1024]{1,0:T(8,128)(2,1)} %shard_map.145.refs_2_.refs_3_), channel_id=1, source_target_pairs={{0,8},{8,0},{16,24},{24,16},{1,9},{9,1},{17,25},{25,17},{2,10},{10... | collective-permute-start | bytes 1572872 | tf_op jit(solution)/shard_map/ppermute | solution.py:43
  2.5 15.5 %collective-permute-start.2 = (bf16[256,1024]{1,0:T(8,128)(2,1)}, bf16[256,1024]{1,0:T(8,128)(2,1)}, u32[]{:S(2)}, u32[]{:S(2)}) collective-permute-start(bf16[256,1024]{1,0:T(8,128)(2,1)} %shard_map.145.refs_2_.refs_3_), channel_id=1, source_target_pairs={{0,16},{8,24},{16,0},{24,8},{1,17},{9,25},{17,1},{25,9},{2,18},{10... | collective-permute-start | bytes 1572872 | tf_op jit(solution)/shard_map/ppermute | solution.py:43
  6.4 5.0 %collective-permute-start.1 = (s32[2,128]{1,0:T(2,128)S(1)}, s32[2,128]{1,0:T(2,128)S(1)}, u32[]{:S(2)}, u32[]{:S(2)}) collective-permute-start(s32[2,128]{1,0:T(2,128)S(1)} %get-tuple-element.37.refs_0_), channel_id=1, source_target_pairs={{0,4},{1,5},{2,6},{3,7},{4,0},{5,1},{6,2},{7,3},{8,12},{9,13},{10,... | collective-permute-start | bytes 3080 | tf_op jit(solution)/shard_map/ppermute | solution.py:43
  9.0 3.2 %collective-permute-start.6 = (s32[2,128]{1,0:T(2,128)S(1)}, s32[2,128]{1,0:T(2,128)S(1)}, u32[]{:S(2)}, u32[]{:S(2)}) collective-permute-start(s32[2,128]{1,0:T(2,128)S(1)} %get-tuple-element.38), channel_id=1, source_target_pairs={{0,8},{8,0},{16,24},{24,16},{1,9},{9,1},{17,25},{25,17},{2,10},{10... | collective-permute-start | bytes 3080 | tf_op jit(solution)/shard_map/ppermute | solution.py:43
  9.0 8.9 %collective-permute-start.7 = (s32[2,128]{1,0:T(2,128)S(1)}, s32[2,128]{1,0:T(2,128)S(1)}, u32[]{:S(2)}, u32[]{:S(2)}) collective-permute-start(s32[2,128]{1,0:T(2,128)S(1)} %get-tuple-element.38), channel_id=1, source_target_pairs={{0,16},{8,24},{16,0},{24,8},{1,17},{9,25},{17,1},{25,9},{2,18},{10... | collective-permute-start | bytes 3080 | tf_op jit(solution)/shard_map/ppermute | solution.py:43
  9.8 8.1 %collective-permute-start.3 = (s32[2,128]{1,0:T(2,128)S(1)}, s32[2,128]{1,0:T(2,128)S(1)}, u32[]{:S(2)}, u32[]{:S(2)}) collective-permute-start(s32[2,128]{1,0:T(2,128)S(1)} %get-tuple-element.37.refs_0_), channel_id=1, source_target_pairs={{0,2},{1,3},{2,0},{3,1},{4,6},{5,7},{6,4},{7,5},{8,10},{9,11},{10,... | collective-permute-start | bytes 3080 | tf_op jit(solution)/shard_map/ppermute | solution.py:43
  11.4 6.5 %collective-permute-start.5 = (s32[2,128]{1,0:T(2,128)S(1)}, s32[2,128]{1,0:T(2,128)S(1)}, u32[]{:S(2)}, u32[]{:S(2)}) collective-permute-start(s32[2,128]{1,0:T(2,128)S(1)} %get-tuple-element.38), channel_id=1, source_target_pairs={{0,24},{8,16},{16,8},{24,0},{1,25},{9,17},{17,9},{25,1},{2,26},{10... | collective-permute-start | bytes 3080 | tf_op jit(solution)/shard_map/ppermute | solution.py:43
  12.2 5.7 %collective-permute-start.4 = (s32[2,128]{1,0:T(2,128)S(1)}, s32[2,128]{1,0:T(2,128)S(1)}, u32[]{:S(2)}, u32[]{:S(2)}) collective-permute-start(s32[2,128]{1,0:T(2,128)S(1)} %collective-permute-done.1.refs_4_.refs_2_), channel_id=1, source_target_pairs={{0,2},{1,3},{2,0},{3,1},{4,6},{5,7},{6,4},{7,5},{8,10},{9,11},{10,... | collective-permute-start | bytes 3080 | tf_op jit(solution)/shard_map/ppermute | solution.py:43
  12.6 1.0 copy-start.6
  13.7 1.0 copy-start.7
  17.9 2.2 %collective-permute-start.8 = (bf16[256,1024]{1,0:T(8,128)(2,1)}, bf16[256,1024]{1,0:T(8,128)(2,1)S(1)}, u32[]{:S(2)}, u32[]{:S(2)}) collective-permute-start(bf16[256,1024]{1,0:T(8,128)(2,1)} %shard_map.149.refs_5_.refs_12_), channel_id=1, source_target_pairs={{0,8},{8,0},{16,24},{24,16},{1,9},{9,1},{17,25},{25,17},{2,10},{10... | collective-permute-start | bytes 1572872 | tf_op jit(solution)/shard_map/ppermute | solution.py:43
  24.1 15.2 %collective-permute-start.13 = (bf16[128,1024]{1,0:T(8,128)(2,1)S(1)}, bf16[128,1024]{1,0:T(8,128)(2,1)S(1)}, u32[]{:S(2)}, u32[]{:S(2)}) collective-permute-start(bf16[128,1024]{1,0:T(8,128)(2,1)S(1)} %get-tuple-element.45.refs_5_.refs_3_), channel_id=1, source_target_pairs={{0,4},{1,5},{2,6},{3,7},{4,0},{5,1},{6,2},{7,3},{8,12},{9,13},{10,... | collective-permute-start | bytes 786440 | tf_op jit(solution)/shard_map/ppermute | solution.py:43
  27.0 12.9 %collective-permute-start.12 = (bf16[128,1024]{1,0:T(8,128)(2,1)S(1)}, bf16[128,1024]{1,0:T(8,128)(2,1)S(1)}, u32[]{:S(2)}, u32[]{:S(2)}) collective-permute-start(bf16[128,1024]{1,0:T(8,128)(2,1)S(1)} %get-tuple-element.45.refs_5_.refs_3_), channel_id=1, source_target_pairs={{0,2},{1,3},{2,0},{3,1},{4,6},{5,7},{6,4},{7,5},{8,10},{9,11},{10,... | collective-permute-start | bytes 786440 | tf_op jit(solution)/shard_map/ppermute | solution.py:43
  28.6 20.1 %collective-permute-start.10 = (bf16[256,1024]{1,0:T(8,128)(2,1)S(1)}, bf16[256,1024]{1,0:T(8,128)(2,1)S(1)}, u32[]{:S(2)}, u32[]{:S(2)}) collective-permute-start(bf16[256,1024]{1,0:T(8,128)(2,1)S(1)} %shard_map.151.refs_7_.refs_4_), channel_id=1, source_target_pairs={{0,16},{8,24},{16,0},{24,8},{1,17},{9,25},{17,1},{25,9},{2,18},{10... | collective-permute-start | bytes 1572872 | tf_op jit(solution)/shard_map/ppermute | solution.py:43
  30.1 18.6 %collective-permute-start.11 = (bf16[256,1024]{1,0:T(8,128)(2,1)S(1)}, bf16[256,1024]{1,0:T(8,128)(2,1)S(1)}, u32[]{:S(2)}, u32[]{:S(2)}) collective-permute-start(bf16[256,1024]{1,0:T(8,128)(2,1)S(1)} %shard_map.151.refs_7_.refs_4_), channel_id=1, source_target_pairs={{0,0},{8,16},{16,8},{24,24},{1,1},{9,17},{17,9},{25,25},{2,2},{10,... | collective-permute-start | bytes 1572872 | tf_op jit(solution)/shard_map/ppermute | solution.py:585
  30.9 17.8 %collective-permute-start.9 = (bf16[256,1024]{1,0:T(8,128)(2,1)S(1)}, bf16[256,1024]{1,0:T(8,128)(2,1)S(1)}, u32[]{:S(2)}, u32[]{:S(2)}) collective-permute-start(bf16[256,1024]{1,0:T(8,128)(2,1)S(1)} %shard_map.151.refs_7_.refs_4_), channel_id=1, source_target_pairs={{0,8},{8,0},{16,24},{24,16},{1,9},{9,1},{17,25},{25,17},{2,10},{10... | collective-permute-start | bytes 1572872 | tf_op jit(solution)/shard_map/ppermute | solution.py:43
  39.3 7.7 %collective-permute-start.14 = (bf16[128,1024]{1,0:T(8,128)(2,1)S(1)}, bf16[128,1024]{1,0:T(8,128)(2,1)S(1)}, u32[]{:S(2)}, u32[]{:S(2)}) collective-permute-start(bf16[128,1024]{1,0:T(8,128)(2,1)S(1)} %collective-permute-done.13.refs_1_.refs_5_), channel_id=1, source_target_pairs={{0,2},{1,3},{2,0},{3,1},{4,6},{5,7},{6,4},{7,5},{8,10},{9,11},{10,... | collective-permute-start | bytes 786440 | tf_op jit(solution)/shard_map/ppermute | solution.py:43
  39.9 8.8 %copy-start.9 = (bf16[1024,8]{0,1:T(8,128)(2,1)S(1)}, bf16[1024,8]{0,1:T(8,128)(2,1)}, u32[]{:S(2)}) copy-start(bf16[1024,8]{0,1:T(8,128)(2,1)} %param.22) | copy-start | bytes 49156
  39.9 17.3 %copy-start.2 = (bf16[1,1408,1024]{2,1,0:T(8,128)(2,1)S(1)}, bf16[1,1408,1024]{2,1,0:T(8,128)(2,1)}, u32[]{:S(2)}) copy-start(bf16[1,1408,1024]{2,1,0:T(8,128)(2,1)} %refs_3_.7) | copy-start | bytes 8650756
  40.4 16.9 %collective-permute-start.18 = (bf16[160,1024]{1,0:T(8,128)(2,1)S(1)}, bf16[160,1024]{1,0:T(8,128)(2,1)S(1)}, u32[]{:S(2)}, u32[]{:S(2)}) collective-permute-start(bf16[160,1024]{1,0:T(8,128)(2,1)S(1)} %get-tuple-element.54), channel_id=1, source_target_pairs={{0,1},{1,0},{2,3},{3,2},{4,5},{5,4},{6,7},{7,6},{8,9},{9,8},{10,11... | collective-permute-start | bytes 983048 | tf_op jit(solution)/shard_map/ppermute | solution.py:43
  47.0 10.3 %copy-start.1 = (bf16[1,1024,1408]{2,1,0:T(8,128)(2,1)S(1)}, bf16[1,1024,1408]{2,1,0:T(8,128)(2,1)}, u32[]{:S(2)}) copy-start(bf16[1,1024,1408]{2,1,0:T(8,128)(2,1)} %refs_2_.7) | copy-start | bytes 8650756
  47.3 10.0 %copy-start = (bf16[1,1024,1408]{2,1,0:T(8,128)(2,1)S(1)}, bf16[1,1024,1408]{2,1,0:T(8,128)(2,1)}, u32[]{:S(2)}) copy-start(bf16[1,1024,1408]{2,1,0:T(8,128)(2,1)} %refs_1_.3) | copy-start | bytes 8650756
  47.3 10.0 %collective-permute-start.19 = (bf16[160,1024]{1,0:T(8,128)(2,1)S(1)}, bf16[160,1024]{1,0:T(8,128)(2,1)S(1)}, u32[]{:S(2)}, u32[]{:S(2)}) collective-permute-start(bf16[160,1024]{1,0:T(8,128)(2,1)S(1)} %shard_map.153.refs_13_), channel_id=1, source_target_pairs={{0,1},{1,0},{2,3},{3,2},{4,5},{5,4},{6,7},{7,6},{8,9},{9,8},{10,11... | collective-permute-start | bytes 983048 | tf_op jit(solution)/shard_map/ppermute | solution.py:43
  52.4 13.3 %collective-permute-start.15 = (bf16[80,1024]{1,0:T(8,128)(2,1)S(1)}, bf16[80,1024]{1,0:T(8,128)(2,1)S(1)}, u32[]{:S(2)}, u32[]{:S(2)}) collective-permute-start(bf16[80,1024]{1,0:T(8,128)(2,1)S(1)} %get-tuple-element.50), channel_id=1, source_target_pairs={{0,6},{1,7},{2,4},{3,5},{4,2},{5,3},{6,0},{7,1},{8,14},{9,15},{10,... | collective-permute-start | bytes 491528 | tf_op jit(solution)/shard_map/ppermute | solution.py:43
  56.6 12.9 %collective-permute-start.16 = (bf16[80,1024]{1,0:T(8,128)(2,1)S(1)}, bf16[80,1024]{1,0:T(8,128)(2,1)S(1)}, u32[]{:S(2)}, u32[]{:S(2)}) collective-permute-start(bf16[80,1024]{1,0:T(8,128)(2,1)S(1)} %get-tuple-element.51), channel_id=1, source_target_pairs={{0,4},{1,5},{2,6},{3,7},{4,0},{5,1},{6,2},{7,3},{8,12},{9,13},{10,... | collective-permute-start | bytes 491528 | tf_op jit(solution)/shard_map/ppermute | solution.py:43
  56.6 12.9 %collective-permute-start.17 = (bf16[80,1024]{1,0:T(8,128)(2,1)S(1)}, bf16[80,1024]{1,0:T(8,128)(2,1)S(1)}, u32[]{:S(2)}, u32[]{:S(2)}) collective-permute-start(bf16[80,1024]{1,0:T(8,128)(2,1)S(1)} %get-tuple-element.52), channel_id=1, source_target_pairs={{0,2},{1,3},{2,0},{3,1},{4,6},{5,7},{6,4},{7,5},{8,10},{9,11},{10,... | collective-permute-start | bytes 491528 | tf_op jit(solution)/shard_map/ppermute | solution.py:43
  60.6 9.5 %collective-permute-start.20 = (bf16[160,1024]{1,0:T(8,128)(2,1)S(1)}, bf16[160,1024]{1,0:T(8,128)(2,1)S(1)}, u32[]{:S(2)}, u32[]{:S(2)}) collective-permute-start(bf16[160,1024]{1,0:T(8,128)(2,1)S(1)} %get-tuple-element.58), channel_id=1, source_target_pairs={{0,1},{1,0},{2,3},{3,2},{4,5},{5,4},{6,7},{7,6},{8,9},{9,8},{10,11... | collective-permute-start | bytes 983048 | tf_op jit(solution)/shard_map/ppermute | solution.py:43
  69.6 8.8 %collective-permute-start.21 = (bf16[160,1024]{1,0:T(8,128)(2,1)S(1)}, bf16[160,1024]{1,0:T(8,128)(2,1)S(1)}, u32[]{:S(2)}, u32[]{:S(2)}) collective-permute-start(bf16[160,1024]{1,0:T(8,128)(2,1)S(1)} %shard_map.157.refs_4_), channel_id=1, source_target_pairs={{0,1},{1,0},{2,3},{3,2},{4,5},{5,4},{6,7},{7,6},{8,9},{9,8},{10,11... | collective-permute-start | bytes 983048 | tf_op jit(solution)/shard_map/ppermute | solution.py:43
  70.9 7.8 %collective-permute-start.22 = (bf16[128,1024]{1,0:T(8,128)(2,1)S(1)}, bf16[128,1024]{1,0:T(8,128)(2,1)S(1)}, u32[]{:S(2)}, u32[]{:S(2)}) collective-permute-start(bf16[128,1024]{1,0:T(8,128)(2,1)S(1)} %get-tuple-element.60), channel_id=1, source_target_pairs={{0,2},{1,3},{2,0},{3,1},{4,6},{5,7},{6,4},{7,5},{8,10},{9,11},{10,... | collective-permute-start | bytes 786440 | tf_op jit(solution)/shard_map/ppermute | solution.py:43
  78.4 10.6 %collective-permute-start.24 = (bf16[160,1024]{1,0:T(8,128)(2,1)S(1)}, bf16[160,1024]{1,0:T(8,128)(2,1)S(1)}, u32[]{:S(2)}, u32[]{:S(2)}) collective-permute-start(bf16[160,1024]{1,0:T(8,128)(2,1)S(1)} %shard_map.160.refs_2_), channel_id=1, source_target_pairs={{0,1},{1,0},{2,3},{3,2},{4,5},{5,4},{6,7},{7,6},{8,9},{9,8},{10,11... | collective-permute-start | bytes 983048 | tf_op jit(solution)/shard_map/ppermute | solution.py:43
  80.5 12.7 %collective-permute-start.23 = (bf16[160,1024]{1,0:T(8,128)(2,1)S(1)}, bf16[160,1024]{1,0:T(8,128)(2,1)S(1)}, u32[]{:S(2)}, u32[]{:S(2)}) collective-permute-start(bf16[160,1024]{1,0:T(8,128)(2,1)S(1)} %shard_map.162.refs_4_), channel_id=1, source_target_pairs={{0,1},{1,0},{2,3},{3,2},{4,5},{5,4},{6,7},{7,6},{8,9},{9,8},{10,11... | collective-permute-start | bytes 983048 | tf_op jit(solution)/shard_map/ppermute | solution.py:43
  82.3 15.4 %collective-permute-start.28 = (bf16[128,1024]{1,0:T(8,128)(2,1)S(1)}, bf16[128,1024]{1,0:T(8,128)(2,1)S(1)}, u32[]{:S(2)}, u32[]{:S(2)}) collective-permute-start(bf16[128,1024]{1,0:T(8,128)(2,1)S(1)} %shard_map.161.refs_4_), channel_id=1, source_target_pairs={{0,4},{1,5},{2,6},{3,7},{4,0},{5,1},{6,2},{7,3},{8,12},{9,13},{10,... | collective-permute-start | bytes 786440 | tf_op jit(solution)/shard_map/ppermute | solution.py:43
  89.8 14.1 %collective-permute-start.29 = (bf16[128,1024]{1,0:T(8,128)(2,1)S(1)}, bf16[128,1024]{1,0:T(8,128)(2,1)S(1)}, u32[]{:S(2)}, u32[]{:S(2)}) collective-permute-start(bf16[128,1024]{1,0:T(8,128)(2,1)S(1)} %get-tuple-element.66), channel_id=1, source_target_pairs={{0,2},{1,3},{2,0},{3,1},{4,6},{5,7},{6,4},{7,5},{8,10},{9,11},{10,... | collective-permute-start | bytes 786440 | tf_op jit(solution)/shard_map/ppermute | solution.py:43
  93.2 10.6 %collective-permute-start.25 = (bf16[80,1024]{1,0:T(8,128)(2,1)S(1)}, bf16[80,1024]{1,0:T(8,128)(2,1)S(1)}, u32[]{:S(2)}, u32[]{:S(2)}) collective-permute-start(bf16[80,1024]{1,0:T(8,128)(2,1)S(1)} %get-tuple-element.62), channel_id=1, source_target_pairs={{0,6},{1,7},{2,4},{3,5},{4,2},{5,3},{6,0},{7,1},{8,14},{9,15},{10,... | collective-permute-start | bytes 491528 | tf_op jit(solution)/shard_map/ppermute | solution.py:43
  94.1 13.8 %collective-permute-start.26 = (bf16[80,1024]{1,0:T(8,128)(2,1)S(1)}, bf16[80,1024]{1,0:T(8,128)(2,1)S(1)}, u32[]{:S(2)}, u32[]{:S(2)}) collective-permute-start(bf16[80,1024]{1,0:T(8,128)(2,1)S(1)} %get-tuple-element.63), channel_id=1, source_target_pairs={{0,4},{1,5},{2,6},{3,7},{4,0},{5,1},{6,2},{7,3},{8,12},{9,13},{10,... | collective-permute-start | bytes 491528 | tf_op jit(solution)/shard_map/ppermute | solution.py:43
  94.9 13.0 %collective-permute-start.27 = (bf16[80,1024]{1,0:T(8,128)(2,1)S(1)}, bf16[80,1024]{1,0:T(8,128)(2,1)S(1)}, u32[]{:S(2)}, u32[]{:S(2)}) collective-permute-start(bf16[80,1024]{1,0:T(8,128)(2,1)S(1)} %get-tuple-element.64), channel_id=1, source_target_pairs={{0,2},{1,3},{2,0},{3,1},{4,6},{5,7},{6,4},{7,5},{8,10},{9,11},{10,... | collective-permute-start | bytes 491528 | tf_op jit(solution)/shard_map/ppermute | solution.py:43
